TPU v7x, 512 devices: a whole 4x4x16 slice. The times are simulated.
512 devices in a mesh: blk: 16 (over z_hi, x, core), rep: 32 (over y, z_lo).
Axes of the slice: x: 4, y: 4, z: 16 (z_hi: 2, z_lo: 8; z = z_hi * 8 + z_lo), core: 2. Of those that a mesh axis runs over, the one named last changes fastest.
Arguments:
- features_t: bfloat16 [1024, 16384], P('rep', 'blk'), may hold values from -6 to 6
- tile_dst: int32 [1024], P('blk'), may hold values from 0 to 7, as said below
- tile_src: int32 [1024], P('blk'), may hold values from 0 to 127, as said below
- tile_edges: int32 [1024], P('blk'), may hold values from 0 to 16384, as said below
- tile_values: bfloat16 [1024, 128, 128], P('blk'), may hold values from -0.5 to 0.5
- weight: bfloat16 [1024, 1024], P('rep'), may hold values from -0.1875 to 0.1875
- cotangent: bfloat16 [1024, 16384], P('rep', 'blk'), may hold values from -6 to 6
Outputs:
- activated: bfloat16 [1024, 16384], P('rep', 'blk')
- grad_weight: float32 [1024, 1024], P('rep')
- grad_features: bfloat16 [1024, 16384], P('rep', 'blk')
Inputs may be any that keep to these rules, and one draw needn't show every extreme that they name: In each group of 64 slots the live slots (tile_edges > 0) come first; the first 8 slots of group g are live with tile_dst b and tile_src g * 8 + b; a group has 8 to 64 live slots, and some group has all 64 live; empty slots have tile_dst 0. Empty slots have tile_src 0. Live slots of group g after the first 8 name source blocks of other groups; for any group g and any other group h at most 4 live slots of g name blocks of h, and in the group with all 64 slots live some h is named by exactly 4. `tile_edges`: zero exactly on empty slots.
All inputs are finite; a program needn't handle non-finite values.
Results may differ from a plain program's by a relative error of at most 0.006.
Values may be sent and summed in bfloat16 or wider, within the bound.
A program may use at most 64 MiB of HBM per device.

v0:
```python
import jax
import jax.numpy as jnp
from jax import lax
from jax.sharding import PartitionSpec as P


def on_device(features_t, tile_dst, tile_src, tile_edges, tile_values, weight, cotangent):
    local_cols = features_t.shape[0]
    rows_dev = features_t.shape[1]
    blk_size = tile_values.shape[1]
    own_blocks = rows_dev // blk_size
    onehot = (tile_dst[None, :] == jnp.arange(own_blocks, dtype=jnp.int32)[:, None]).astype(
        jnp.float32
    )
    weights = tile_edges.astype(jnp.float32)
    totals = jnp.sum(onehot * weights[None, :], axis=1)
    mixing = onehot * weights[None, :] / totals[:, None]
    coef = jnp.sum(mixing, axis=0)
    whole = lax.all_gather(features_t, "blk", axis=1, tiled=True)
    all_blocks = whole.shape[1] // blk_size
    picked = jnp.take(whole.reshape(local_cols, all_blocks, blk_size), tile_src, axis=1)
    contrib = jnp.einsum("ctk,tjk->tcj", picked, tile_values, preferred_element_type=jnp.float32)
    summed = jnp.einsum("bt,tcj->cbj", mixing, contrib, precision=lax.Precision.HIGHEST)
    aggregated = summed.reshape(local_cols, rows_dev).astype(jnp.bfloat16)
    columns = lax.all_to_all(weight, "rep", split_axis=1, concat_axis=0, tiled=True)
    part_w = columns
    pre = lax.dot_general(
        part_w,
        lax.all_gather(aggregated, "rep", axis=0, tiled=True),
        (((0,), (0,)), ((), ())),
        preferred_element_type=jnp.float32,
    )
    sig = jax.nn.sigmoid(pre)
    activated = (pre * sig).astype(jnp.bfloat16)
    grad_pre = (cotangent.astype(jnp.float32) * sig * (1.0 + pre * (1.0 - sig))).astype(
        jnp.bfloat16
    )
    piece = lax.all_gather(grad_pre, "rep", axis=0, tiled=True)
    block_w = lax.dot_general(
        aggregated, piece, (((1,), (1,)), ((), ())), preferred_element_type=jnp.float32
    )
    partial_w = block_w
    part_w = weight
    partial_y = jnp.dot(part_w, piece, preferred_element_type=jnp.float32)
    partial_w, partial_y = (partial_w, partial_y)
    grad_weight = lax.psum(partial_w, "blk")
    grad_agg = partial_y.astype(jnp.bfloat16)
    grad_blocks = grad_agg.reshape(local_cols, own_blocks, blk_size)
    chosen = jnp.take(grad_blocks, tile_dst, axis=1)
    back = jnp.einsum("ctj,tjk->tck", chosen, tile_values, preferred_element_type=jnp.float32)
    back = back * coef[:, None, None]
    buffer = jax.ops.segment_sum(back, tile_src, num_segments=all_blocks)
    mine = lax.psum_scatter(buffer, "blk", scatter_dimension=0, tiled=True)
    grad_features = mine.transpose(1, 0, 2).reshape(local_cols, rows_dev).astype(jnp.bfloat16)
    return (activated, grad_weight, grad_features)


def solution(mesh):
    in_specs = (
        P("rep", "blk"),
        P("blk"),
        P("blk"),
        P("blk"),
        P("blk", None, None),
        P("rep", None),
        P("rep", "blk"),
    )
    out_specs = (P("rep", "blk"), P("rep", None), P("rep", "blk"))
    return jax.shard_map(
        on_device, mesh=mesh, in_specs=in_specs, out_specs=out_specs, check_vma=False
    )
```

profile of v0, /device:TPU:1, one launch (start us, length us, event | category | flops | bytes accessed | tf_op | source)
XLA Modules:
  0.0 939.9 jit_solution(16078078234473379701)
XLA Ops:
  7.2 0.0 copy-start
  7.2 0.0 all-gather.4.cloned.1.call-start
  7.2 0.7 all-gather.4.cloned.1.call-update
  7.9 0.0 all-gather.6.cloned.1.call-start
  8.0 0.7 convert_element_type.37
  8.6 0.7 compare_select_fusion.1
  9.3 0.8 select_reduce_fusion
  10.1 0.7 compare_and_fusion.1
  10.7 84.2 %all-gather.4.cloned.1.call-done = bf16[32,16384]{1,0:T(8,128)(2,1)} async-done(((bf16[32,1024]{1,0:T(8,128)(2,1)}), bf16[32,16384]{1,0:T(8,128)(2,1)}) %all-gather.4.cloned.1.call-update) | async-done | bytes 1048592 | tf_op jit(solution)/shard_map/all_gather | solution.py:19
  94.9 1.4 copy_bitcast_fusion
  96.3 1.4 gather_fusion
  97.7 0.0 copy-done
  97.7 0.0 copy-start.3
  97.7 0.0 copy-start.1
  97.7 2.3 fusion.3
  100.0 0.0 copy-done.3
  100.0 0.0 copy-start.2
  100.0 1.3 convolution_convert_fusion
  101.3 0.6 copy.34
  101.9 0.0 all-gather.6.cloned.1.call-update
  102.0 0.0 all-gather.8.cloned.1.call-start
  102.0 0.0 copy-done.1
  102.0 0.2 copy.19
  102.2 0.2 reshape.63
  102.4 16.1 %all_to_all.19 = bf16[32,2,512]{2,1,0:T(2,128)(2,1)S(1)} all-to-all(bf16[32,2,512]{2,1,0:T(2,128)(2,1)S(1)} %reshape.63), channel_id=1, replica_groups=mesh['blk'=16,'rep'=32] {'rep'}, dimensions={0} | all-to-all | bytes 131072 | tf_op jit(solution)/shard_map/all_to_all | solution.py:25
  118.5 0.2 reshape.64
  118.8 0.1 copy.20
  118.9 0.3 all_to_all.17
  119.1 179.7 %all-gather.6.cloned.1.call-done = bf16[1024,1024]{1,0:T(8,128)(2,1)} async-done(((bf16[32,1024]{1,0:T(8,128)(2,1)}), bf16[1024,1024]{1,0:T(8,128)(2,1)}) %all-gather.6.cloned.1.call-update) | async-done | bytes 2097168 | tf_op jit(solution)/shard_map/all_gather | solution.py:29
  298.9 0.0 copy-done.2
  298.9 2.8 multiply_convert_fusion
  301.6 0.0 all-gather.8.cloned.1.call-update
  301.6 0.0 reduce-scatter.2.cloned.1.call-start
  301.7 0.1 fusion.12
  301.8 225.9 %all-gather.8.cloned.1.call-done = bf16[1024,1024]{1,0:T(8,128)(2,1)} async-done(((bf16[32,1024]{1,0:T(8,128)(2,1)}), bf16[1024,1024]{1,0:T(8,128)(2,1)}) %all-gather.8.cloned.1.call-update) | async-done | bytes 2097168 | tf_op jit(solution)/shard_map/all_gather | solution.py:38
  527.7 2.1 fusion
  529.8 1.4 gather_fusion.1
  531.2 0.0 copy-start.4
  531.2 1.8 convolution_multiply_fusion
  533.0 1.6 broadcast_in_dim.37
  534.6 0.0 copy-done.4
  534.6 9.3 scatter_fusion
  543.9 0.0 reduce-scatter.2.cloned.1.call-update
  543.9 0.0 all-reduce.2.cloned.1.call-start
  544.0 3.0 fusion.20
  546.9 0.0 all-reduce.2.cloned.1.call-update
  547.0 135.7 %reduce-scatter.2.cloned.1.call-done = f32[8,32,128]{2,1,0:T(8,128)} async-done(((f32[128,32,128]{2,1,0:T(8,128)}), f32[8,32,128]{2,1,0:T(8,128)}) %reduce-scatter.2.cloned.1.call-update) | async-done | bytes 131088 | tf_op jit(solution)/shard_map/reduce_scatter | solution.py:53
  682.6 1.5 copy_bitcast_fusion.2
  684.2 247.6 %all-reduce.2.cloned.1.call-done = f32[32,1024]{1,0:T(8,128)} async-done(((f32[32,1024]{1,0:T(8,128)}), f32[32,1024]{1,0:T(8,128)}) %all-reduce.2.cloned.1.call-update) | async-done | bytes 131088 | tf_op jit(solution)/shard_map/psum | solution.py:46
  931.8 1.6 copy.38
  (6 shorter events, 0.1 us)
Async XLA Ops:
  7.2 90.5 %copy-start = (bf16[64,128,128]{2,1,0:T(8,128)(2,1)S(1)}, bf16[64,128,128]{2,1,0:T(8,128)(2,1)}, u32[]{:S(2)}) copy-start(bf16[64,128,128]{2,1,0:T(8,128)(2,1)} %param.11) | copy-start | bytes 6291460
  7.2 87.7 %all-gather.4.cloned.1.call-start = ((), (), s32[]{:S(2)}) async-start(), calls=%async_computation.2 | async-start | bytes 1114112 | tf_op jit(solution)/shard_map/all_gather | solution.py:19
  7.9 290.9 %all-gather.6.cloned.1.call-start = ((), (), s32[]{:S(2)}) async-start(), calls=%async_computation.3 | async-start | bytes 2162688 | tf_op jit(solution)/shard_map/all_gather | solution.py:29
  97.7 2.3 copy-start.3
  97.7 4.3 copy-start.1
  100.0 198.8 %copy-start.2 = (bf16[32,1024]{1,0:T(8,128)(2,1)S(1)}, bf16[32,1024]{1,0:T(8,128)(2,1)}, u32[]{:S(2)}) copy-start(bf16[32,1024]{1,0:T(8,128)(2,1)} %param.13) | copy-start | bytes 196612
  102.0 425.7 %all-gather.8.cloned.1.call-start = ((), (), s32[]{:S(2)}) async-start(), calls=%async_computation.4 | async-start | bytes 2162688 | tf_op jit(solution)/shard_map/all_gather | solution.py:38
  301.6 381.0 %reduce-scatter.2.cloned.1.call-start = ((), (), s32[]{:S(2)}) async-start(), calls=%async_computation.6 | async-start | bytes 2228224 | tf_op jit(solution)/shard_map/reduce_scatter | solution.py:53
  531.2 3.4 copy-start.4
  543.9 387.9 %all-reduce.2.cloned.1.call-start = ((), (), s32[]{:S(2)}) async-start(), calls=%async_computation.5 | async-start | bytes 262144 | tf_op jit(solution)/shard_map/psum | solution.py:46
Sparse Core Ops, SparseCore 0:
  11.4 83.4 all-gather.3
  102.1 196.7 all-gather.5
  301.8 225.8 all-gather.7
  544.0 138.5 reduce-scatter.1
  685.9 245.8 all-reduce.1
where the time goes:
time: 941 us; the launch traced here: 940 us
  waiting for transfers between devices  874 us (93%)
  blocking collectives  16.1 us (2%)
  between operations  13.9 us (1%)
  other arithmetic  13.7 us (1%)
  matrix products  13.1 us (1%)
    psum x1, waiting for transfers between devices, on_device(): grad_weight = lax.psum(partial_w, 'blk')  248 us
    all_gather x1, waiting for transfers between devices, on_device(): piece = lax.all_gather(grad_pre, 'rep', axis=0, tiled=True)  226 us
    all_gather x1, waiting for transfers between devices, on_device(): lax.all_gather(aggregated, 'rep', axis=0, tiled=True)  180 us
    reduce_scatter x1, waiting for transfers between devices, on_device(): mine = lax.psum_scatter(buffer, 'blk', scatter_dimension=0, tiled=True)  136 us
    all_gather x1, waiting for transfers between devices, on_device(): whole = lax.all_gather(features_t, 'blk', axis=1, tiled=True)  84.2 us
  transfers between devices with their start and end apart: 5, of which 5 were waited for; matrix products, arithmetic and copies ran while one was open for 1% of the time, Pallas kernels for 0%

commit v1 on v0

v1 whole, which is shorter than its diff:
```python
import functools

import jax
import jax.numpy as jnp
from jax import lax
from jax.experimental import pallas as pl
from jax.experimental.pallas import tpu as pltpu
from jax.sharding import PartitionSpec as P

FULL = dict(ZH=2, X=4, C=2, Y=4, ZL=8)
PER = 4
MESH = pl.DeviceIdType.MESH
BF = jnp.bfloat16
F32 = jnp.float32


def dot(a, b, ca, cb):
    return lax.dot_general(a, b, (((ca,), (cb,)), ((), ())), preferred_element_type=F32)


def shapes(cfg, rb, tb, nt):
    X, C, Y, ZL = cfg["X"], cfg["C"], cfg["Y"], cfg["ZL"]
    Q = X * C
    F = rb * Y * ZL
    qw = F // Q
    qy = Q // Y
    bpd = ZL
    x1, y1, z1 = max(X - 1, 1), max(Y - 1, 1), max(ZL - 1, 1)
    nk = -(-cfg["ZH"] * Q * PER // 128) * 128
    bufs = dict(
        fv=((rb, bpd * tb), BF),
        wv=((rb, F), BF),
        cv=((rb, bpd * tb), BF),
        dv=((1, nt), jnp.int32),
        sv=((1, nt), jnp.int32),
        ev=((1, nt), jnp.int32),
        itv=((8, nk), jnp.int32),
        ftv=((2 * bpd + 8, nk), F32),
        gown=((Q * bpd, rb, tb), BF),
        goth=((Q * bpd, rb, tb), BF),
        tv=((nt, tb, tb), BF),
        wb=((Q, rb, qw), BF),
        wg=((Q, ZL, rb, qw), BF),
        cb=((bpd, rb, tb), BF),
        ct=((ZL, rb, tb), BF),
        aggb=((bpd, rb, tb), BF),
        A=((ZL, rb, tb), BF),
        pps=((y1, qy, qw, tb), BF),
        ppr=((y1, qy, qw, tb), BF),
        GP=((Q, qw, tb), BF),
        actb=((ZL, rb, tb), BF),
        actr=((bpd, rb, tb), BF),
        gab=((ZL, rb, tb), BF),
        GA=((bpd, rb, tb), BF),
        PS=((X, ZL, rb, qw), BF),
        PO=((X, ZL, rb, qw), F32),
        PR=((X, ZL, rb, qw), BF),
        DXs=((x1, ZL, rb, qw), BF),
        DXr=((x1, ZL, rb, qw), BF),
        Sb=((ZL, rb, qw), BF),
        S32=((ZL, rb, qw), F32),
        DZr=((z1, rb, qw), BF),
        Ts=((rb, qw), F32),
        Tr=((rb, qw), F32),
        OutW=((Q, rb, qw), F32),
        Dsib0=((X, bpd, rb, tb), BF),
        Dsib1=((X, bpd, rb, tb), BF),
        Drec0=((X, bpd, rb, tb), BF),
        Drec1=((X, bpd, rb, tb), BF),
        Dkeep0=((X, bpd, rb, tb), F32),
        Dkeep1=((X, bpd, rb, tb), F32),
        EXs0=((x1, bpd, rb, tb), BF),
        EXs1=((x1, bpd, rb, tb), BF),
        EXr0=((x1, bpd, rb, tb), BF),
        EXr1=((x1, bpd, rb, tb), BF),
        FZs=((bpd, rb, tb), BF),
        FZr=((bpd, rb, tb), BF),
    )
    sems = dict(
        fz=1, fx0=x1, fx1=x1, fc0=X, fc1=X, w1=z1, w2=x1, w3=X, ct=z1, ag=z1, pp=y1, gp=y1, act=z1, ga=z1,
        p=1, dx=x1, dz=z1, dt=1, ow=2 * X, d0=1, d1=1, e0=x1, e1=x1, gz=1,
    )
    smem = dict(itab=((8, nk), jnp.int32), ftab=((2 * bpd + 8, nk), F32))
    return bufs, sems, smem


def tables(bpd, dst, src, edges, itv, ftv):
    nt = dst.shape[1]
    nk = itv.shape[1]
    r0 = lax.broadcasted_iota(jnp.int32, (nt, nt), 0)
    r1 = lax.broadcasted_iota(jnp.int32, (nt, nt), 1)
    k1 = lax.broadcasted_iota(jnp.int32, (nt, nk), 1)
    t0 = lax.broadcasted_iota(jnp.int32, (nt, nk), 0)
    lane = lax.broadcasted_iota(jnp.int32, (1, nt), 1)

    def column(row):
        return jnp.sum(jnp.where(r0 == r1, row, jnp.zeros_like(row)), axis=1, keepdims=True)

    bits = bpd.bit_length() - 1
    group = jnp.where((edges > 0) & (lane >= bpd), lax.shift_right_logical(src, bits), -1)
    group_c = column(group)
    rank = jnp.sum(jnp.where((group_c == group) & (r1 < r0), 1, 0), axis=1, keepdims=True)
    pick = jnp.where(group_c >= 0, group_c * PER + rank, -1) == k1

    def by_k(col):
        return jnp.sum(jnp.where(pick, col, jnp.zeros_like(col)), axis=0, keepdims=True)

    at_src, at_dst = by_k(column(src & (bpd - 1))), by_k(column(dst))
    itv[0:1] = by_k(t0)
    itv[1:2] = at_src
    itv[2:3] = at_dst
    blocks = lax.broadcasted_iota(jnp.int32, (bpd, nt), 0)
    weights = jnp.where(dst == blocks, edges.astype(F32), 0.0)
    coef = jnp.sum(weights / jnp.sum(weights, axis=1, keepdims=True), axis=0, keepdims=True)
    coef_k = by_k(column(coef))
    blocks = lax.broadcasted_iota(jnp.int32, (bpd, nk), 0)
    ftv[0:bpd] = jnp.where(at_dst == blocks, coef_k, 0.0)
    ftv[bpd:2 * bpd] = jnp.where(at_src == blocks, coef_k, 0.0)
    ftv[2 * bpd:2 * bpd + 1, 0:nt] = coef


def body(cfg, buf_names, sem_names, feat_hbm, tv_hbm, w_hbm, cot_hbm, dst_hbm, src_hbm, edge_hbm, act_o, gw_o, gf_o, *scr):
    ZH, X, C, Y, ZL = cfg["ZH"], cfg["X"], cfg["C"], cfg["Y"], cfg["ZL"]
    nb, ns = len(buf_names), len(sem_names)
    B = dict(zip(buf_names, scr[:nb]))
    SS = dict(zip(sem_names, scr[nb:nb + ns]))
    RS = dict(zip(sem_names, scr[nb + ns:nb + 2 * ns]))
    load_sem, itab, ftab = scr[nb + 2 * ns:]
    feat, w, cot = B["fv"], B["wv"], B["cv"]
    Q = X * C
    bpd = ZL
    rb, tb = B["A"].shape[1:]
    qw = B["wb"].shape[2]
    qy = Q // Y
    rows = ZL * rb

    blk, rep = lax.axis_index("blk"), lax.axis_index("rep")
    zh = lax.div(blk, Q)
    me = lax.rem(blk, Q)
    x, c = lax.div(me, C), lax.rem(me, C)
    y, zl = lax.div(rep, ZL), lax.rem(rep, ZL)
    zo, co = 1 - zh, 1 - c

    def dev(zh_=zh, x_=x, c_=c, y_=y, zl_=zl):
        return ((zh_ * X + x_) * C + c_, y_ * ZL + zl_)

    def up(v, d, n):
        return lax.rem(v + d, n)

    def down(v, d, n):
        return lax.rem(v + n - d, n)

    anti, sib = dev(zh_=zo), dev(c_=co)
    sent = []

    def send(src, dst, name, i, to):
        cp = pltpu.make_async_remote_copy(
            src_ref=src, dst_ref=dst, send_sem=SS[name].at[i], recv_sem=RS[name].at[i],
            device_id=to, device_id_type=MESH,
        )
        cp.start()
        sent.append(cp)

    def got(dst, name, i):
        pltpu.make_async_remote_copy(
            src_ref=dst, dst_ref=dst, send_sem=SS[name].at[i], recv_sem=RS[name].at[i],
            device_id=sib, device_id_type=MESH,
        ).wait_recv()

    loads = [
        pltpu.make_async_copy(a, b, load_sem.at[i])
        for i, (a, b) in enumerate((
            (feat_hbm, feat), (w_hbm, w), (cot_hbm, cot), (tv_hbm, B["tv"]),
            (dst_hbm, B["dv"]), (src_hbm, B["sv"]), (edge_hbm, B["ev"]),
        ))
    ]
    for ld in loads:
        ld.start()

    barrier = pltpu.get_barrier_semaphore()
    partners = [anti]
    partners += [dev(x_=up(x, d, X), c_=(c if e == 0 else co)) for d in range(X) for e in range(C) if d or e]
    partners += [dev(zl_=up(zl, d, ZL)) for d in range(1, ZL)]
    partners += [dev(y_=up(y, d, Y)) for d in range(1, Y)]
    for p in partners:
        pl.semaphore_signal(barrier, inc=1, device_id=p, device_id_type=MESH)

    gown, goth, tv = B["gown"], B["goth"], B["tv"]
    loads[0].wait()
    for b in range(bpd):
        gown[me * bpd + b] = feat[:, b * tb:(b + 1) * tb]
    pl.semaphore_wait(barrier, len(partners))

    def seg(m):
        return pl.ds(m * bpd, bpd)

    mine = seg(me)
    send(gown.at[mine], goth.at[mine], "fz", 0, anti)
    for d in range(1, X):
        send(gown.at[mine], gown.at[mine], "fx0", d - 1, dev(x_=up(x, d, X)))
    send(gown.at[mine], gown.at[mine], "fc0", 0, sib)
    for ld in loads[4:]:
        ld.wait()
    tables(bpd, B["dv"][...], B["sv"][...], B["ev"][...], B["itv"], B["ftv"])
    to_smem = [
        pltpu.make_async_copy(B["itv"], itab, load_sem.at[7]),
        pltpu.make_async_copy(B["ftv"], ftab, load_sem.at[8]),
    ]
    for cp in to_smem:
        cp.start()
    loads[1].wait()
    loads[2].wait()
    for b in range(bpd):
        B["cb"][b] = cot[:, b * tb:(b + 1) * tb]
    for q in range(Q):
        B["wb"][q] = w[:, q * qw:(q + 1) * qw]
    B["wg"][me, zl] = B["wb"][me]
    B["ct"][zl] = B["cb"][zl]
    wg, wb = B["wg"], B["wb"]
    for d in range(1, ZL):
        z = up(zl, d, ZL)
        send(wb.at[me], wg.at[me, zl], "w1", d - 1, dev(zl_=z))
    for d in range(1, X):
        part = gown.at[seg(down(x, d, X) * C + c)]
        got(part, "fx0", d - 1)
        send(part, part, "fc0", d, sib)
    loads[3].wait()
    for cp in to_smem:
        cp.wait()
    acc = tuple(ftab[2 * bpd, b] * dot(gown[me * bpd + b], tv[b], 1, 1) for b in range(bpd))

    def forward(g, half, m, acc):
        acc = list(acc)
        for j in range(PER):
            k = (half * Q + m) * PER + j
            out = dot(g[m * bpd + itab[1, k]], tv[itab[0, k]], 1, 1)
            for b in range(bpd):
                acc[b] = acc[b] + ftab[b, k] * out
        return tuple(acc)

    got(goth.at[mine], "fz", 0)
    for d in range(1, X):
        send(goth.at[mine], goth.at[mine], "fx1", d - 1, dev(x_=up(x, d, X)))
    send(goth.at[mine], goth.at[mine], "fc1", 0, sib)
    for d in range(X):
        got(gown.at[seg(down(x, d, X) * C + co)], "fc0", d)
    acc = lax.fori_loop(1, Q, lambda d, a: forward(gown, zh, lax.rem(me + d, Q), a), acc)
    for d in range(1, X):
        part = goth.at[seg(down(x, d, X) * C + c)]
        got(part, "fx1", d - 1)
        send(part, part, "fc1", d, sib)
    for d in range(1, ZL):
        got(wg.at[me, down(zl, d, ZL)], "w1", d - 1)
    for d in range(1, X):
        send(wg.at[me], wg.at[me], "w2", d - 1, dev(x_=up(x, d, X)))
    send(wg.at[me], wg.at[me], "w3", 0, sib)
    for d in range(X):
        got(goth.at[seg(down(x, d, X) * C + co)], "fc1", d)
    acc = lax.fori_loop(0, Q, lambda m, a: forward(goth, zo, m, a), acc)

    A = B["A"]
    for b in range(bpd):
        B["aggb"][b] = acc[b].astype(BF)
    A[zl] = B["aggb"][zl]
    for d in range(1, ZL):
        z = up(zl, d, ZL)
        send(B["aggb"].at[z], A.at[zl], "ag", d - 1, dev(zl_=z))
    for d in range(1, ZL):
        z = up(zl, d, ZL)
        send(B["cb"].at[z], B["ct"].at[zl], "ct", d - 1, dev(zl_=z))
    for d in range(1, X):
        part = wg.at[down(x, d, X) * C + c]
        got(part, "w2", d - 1)
        send(part, part, "w3", d, sib)
    for d in range(X):
        got(wg.at[down(x, d, X) * C + co], "w3", d)
    for d in range(1, ZL):
        got(A.at[down(zl, d, ZL)], "ag", d - 1)

    a2 = A[...].reshape(rows, tb)

    def pre_part(y_, i):
        return dot(wg[y_ * qy + i].reshape(rows, qw), a2, 0, 0)

    pps, ppr, GP = B["pps"], B["ppr"], B["GP"]
    for d in range(1, Y):
        y_ = up(y, d, Y)
        for i in range(qy):
            pps[d - 1, i] = pre_part(y_, i).astype(BF)
        send(pps.at[d - 1], ppr.at[d - 1], "pp", d - 1, dev(y_=y_))
    pre = jnp.concatenate([pre_part(y, i) for i in range(qy)], axis=0)
    for d in range(1, ZL):
        got(B["ct"].at[down(zl, d, ZL)], "ct", d - 1)
    cotangent = B["ct"][...].reshape(rows, tb).astype(F32)
    for d in range(1, Y):
        got(ppr.at[d - 1], "pp", d - 1)
        pre = pre + ppr[d - 1].reshape(rows, tb).astype(F32)
    sig = jax.nn.sigmoid(pre)
    gp = (cotangent * sig * (1.0 + pre * (1.0 - sig))).astype(BF).reshape(qy, qw, tb)
    for i in range(qy):
        GP[y * qy + i] = gp[i]
    for d in range(1, Y):
        part = GP.at[pl.ds(y * qy, qy)]
        send(part, part, "gp", d - 1, dev(y_=up(y, d, Y)))
    actb, actr = B["actb"], B["actr"]
    actb[...] = (pre * sig).astype(BF).reshape(ZL, rb, tb)
    actr[zl] = actb[zl]
    for d in range(1, ZL):
        z = up(zl, d, ZL)
        send(actb.at[z], actr.at[zl], "act", d - 1, dev(zl_=z))
    for d in range(1, Y):
        got(GP.at[pl.ds(down(y, d, Y) * qy, qy)], "gp", d - 1)

    ga = dot(wg[0].reshape(rows, qw), GP[0], 1, 0)
    for q in range(1, Q):
        ga = ga + dot(wg[q].reshape(rows, qw), GP[q], 1, 0)
    gab, GA = B["gab"], B["GA"]
    gab[...] = ga.astype(BF).reshape(ZL, rb, tb)
    GA[zl] = gab[zl]
    for d in range(1, ZL):
        z = up(zl, d, ZL)
        send(gab.at[z], GA.at[zl], "ga", d - 1, dev(zl_=z))

    PS, PO, PR = B["PS"], B["PO"], B["PR"]
    for i in range(X):
        PS[i] = dot(a2, GP[i * C + co], 1, 1).astype(BF).reshape(ZL, rb, qw)
    send(PS, PR, "p", 0, sib)
    for i in range(X):
        PO[i] = dot(a2, GP[i * C + c], 1, 1).reshape(ZL, rb, qw)
    got(PR, "p", 0)
    DXs, DXr = B["DXs"], B["DXr"]
    for d in range(1, X):
        x_ = up(x, d, X)
        DXs[d - 1] = (PO[x_] + PR[x_].astype(F32)).astype(BF)
        send(DXs.at[d - 1], DXr.at[d - 1], "dx", d - 1, dev(x_=x_))
    for d in range(1, ZL):
        got(GA.at[down(zl, d, ZL)], "ga", d - 1)

    def backward(half, m):
        outs = [None] * bpd
        for j in range(PER):
            k = (half * Q + m) * PER + j
            back = dot(GA[itab[2, k]], tv[itab[0, k]], 1, 0)
            for b in range(bpd):
                term = ftab[bpd + b, k] * back
                outs[b] = term if j == 0 else outs[b] + term
        return outs

    def contribute(half, core, start, stop, at, into):
        def step(i, carry):
            i = at(i)
            for b, out in enumerate(backward(half, i * C + core)):
                into[i, b] = out.astype(into.dtype)
            return carry
        lax.fori_loop(start, stop, step, 0)

    Dsib, Drec, Dkeep = (B["Dsib0"], B["Dsib1"]), (B["Drec0"], B["Drec1"]), (B["Dkeep0"], B["Dkeep1"])
    EXs, EXr = (B["EXs0"], B["EXs1"]), (B["EXr0"], B["EXr1"])

    def to_x(n):
        got(Drec[n], "d%d" % n, 0)
        for d in range(1, X):
            x_ = up(x, d, X)
            EXs[n][d - 1] = (Dkeep[n][x_] + Drec[n][x_].astype(F32)).astype(BF)
            send(EXs[n].at[d - 1], EXr[n].at[d - 1], "e%d" % n, d - 1, dev(x_=x_))

    def from_x(n):
        total = Dkeep[n][x] + Drec[n][x].astype(F32)
        for d in range(1, X):
            got(EXr[n].at[d - 1], "e%d" % n, d - 1)
            total = total + EXr[n][d - 1].astype(F32)
        return total

    contribute(zo, co, 0, X, lambda i: i, Dsib[0])
    send(Dsib[0], Drec[0], "d0", 0, sib)
    contribute(zo, c, 0, X, lambda i: i, Dkeep[0])

    to_x(0)
    S32, Sb, DZr = B["S32"], B["Sb"], B["DZr"]
    total = PO[x] + PR[x].astype(F32)
    for d in range(1, X):
        got(DXr.at[d - 1], "dx", d - 1)
        total = total + DXr[d - 1].astype(F32)
    S32[...] = total
    Sb[...] = total.astype(BF)
    for d in range(1, ZL):
        z = up(zl, d, ZL)
        send(Sb.at[z], DZr.at[d - 1], "dz", d - 1, dev(zl_=z))
    contribute(zh, co, 0, X, lambda i: i, Dsib[1])
    send(Dsib[1], Drec[1], "d1", 0, sib)
    contribute(zh, c, 1, X, lambda i: lax.rem(x + i, X), Dkeep[1])
    for b in range(bpd):
        Dkeep[1][x, b] = ftab[2 * bpd, b] * dot(GA[b], tv[b], 1, 0)
    FZs, FZr = B["FZs"], B["FZr"]
    FZs[...] = from_x(0).astype(BF)
    send(FZs, FZr, "gz", 0, anti)

    total = S32[zl]
    for d in range(1, ZL):
        got(DZr.at[d - 1], "dz", d - 1)
        total = total + DZr[d - 1].astype(F32)
    Ts, Tr, OutW = B["Ts"], B["Tr"], B["OutW"]
    Ts[...] = total
    send(Ts, Tr, "dt", 0, anti)
    to_x(1)
    for d in range(1, ZL):
        got(actr.at[down(zl, d, ZL)], "act", d - 1)
    for b in range(bpd):
        act_o[:, b * tb:(b + 1) * tb] = actr[b]
    got(Tr, "dt", 0)
    OutW[me] = Ts[...] + Tr[...]
    others = [(d, e) for d in range(X) for e in range(C) if d or e]
    for n, (d, e) in enumerate(others):
        to = dev(x_=up(x, d, X), c_=(co if e else c))
        send(OutW.at[me], OutW.at[me], "ow", n, to)
    own = from_x(1)
    for n, (d, e) in enumerate(others):
        got(OutW.at[down(x, d, X) * C + (co if e else c)], "ow", n)
    for q in range(Q):
        gw_o[:, q * qw:(q + 1) * qw] = OutW[q]
    got(FZr, "gz", 0)
    own = (own + FZr[...].astype(F32)).astype(BF)
    for b in range(bpd):
        gf_o[:, b * tb:(b + 1) * tb] = own[b]
    for cp in sent:
        cp.wait_send()


def hand_over(*refs):
    sem = refs[-1]
    n = (len(refs) - 1) // 2
    copies = [pltpu.make_async_copy(refs[i], refs[n + i], sem.at[i]) for i in range(n)]
    for cp in copies:
        cp.start()
    for cp in copies:
        cp.wait()


def on_device(cfg, features_t, tile_dst, tile_src, tile_edges, tile_values, weight, cotangent):
    rb = features_t.shape[0]
    nt, tb = tile_values.shape[:2]
    bufs, sems, smem = shapes(cfg, rb, tb, nt)
    vm, hbm = pl.BlockSpec(memory_space=pltpu.VMEM), pl.BlockSpec(memory_space=pltpu.HBM)
    kernel = functools.partial(body, cfg, tuple(bufs), tuple(sems))
    outs = (
        jax.ShapeDtypeStruct(features_t.shape, BF),
        jax.ShapeDtypeStruct(weight.shape, F32),
        jax.ShapeDtypeStruct(features_t.shape, BF),
    )
    results = pl.pallas_call(
        kernel,
        out_shape=outs,
        in_specs=[hbm] * 7,
        out_specs=(vm, vm, vm),
        scratch_shapes=[pltpu.VMEM(s, t) for s, t in bufs.values()]
        + [pltpu.SemaphoreType.DMA((n,)) for n in sems.values()] * 2
        + [pltpu.SemaphoreType.DMA((9,))]
        + [pltpu.SMEM(s, t) for s, t in smem.values()],
        compiler_params=pltpu.CompilerParams(
            collective_id=0, has_side_effects=True, vmem_limit_bytes=63 * 1024 * 1024
        ),
        name="graph_conv",
    )(features_t, tile_values, weight, cotangent, *(v.reshape(1, nt) for v in (tile_dst, tile_src, tile_edges)))
    return pl.pallas_call(
        hand_over,
        out_shape=outs,
        in_specs=[hbm] * len(outs),
        out_specs=(hbm,) * len(outs),
        scratch_shapes=[pltpu.SemaphoreType.DMA((len(outs),))],
        compiler_params=pltpu.CompilerParams(vmem_limit_bytes=63 * 1024 * 1024),
        name="hand_over",
    )(*results)


def solution(mesh, cfg=None):
    in_specs = (
        P("rep", "blk"),
        P("blk"),
        P("blk"),
        P("blk"),
        P("blk", None, None),
        P("rep", None),
        P("rep", "blk"),
    )
    out_specs = (P("rep", "blk"), P("rep", None), P("rep", "blk"))
    return jax.shard_map(
        functools.partial(on_device, cfg or FULL), mesh=mesh, in_specs=in_specs, out_specs=out_specs, check_vma=False
    )
```

time: 941 us -> 96.3 us (0.10)
  waiting for transfers between devices: 874 us -> 0 us
  Pallas kernels: 0 us -> 95.5 us
  blocking collectives: 16.1 us -> 0 us
  other arithmetic: 13.7 us -> 0 us
  between operations: 13.9 us -> 0.64 us
  matrix products: 13.1 us -> 0 us
    all_gather x3 -> x0, waiting for transfers between devices: 490 us -> none  [the longest x1 226 us: on_device(): piece = lax.all_gather(grad_pre, 'rep', axis=0, tiled=True)]
    psum x1 -> x0, waiting for transfers between devices: 248 us -> none  [on_device(): grad_weight = lax.psum(partial_w, 'blk')]
    reduce_scatter x1 -> x0, waiting for transfers between devices: 136 us -> none  [on_device(): mine = lax.psum_scatter(buffer, 'blk', scatter_dimension=0, tiled=True)]
    pallas_call x0 -> x2, Pallas kernels: none -> 95.5 us  [the longest x1 86.5 us: on_device(): pl.pallas_call(kernel, out_shape=outs, in_specs=[hbm] * 7, out_specs=(vm,...]
    all_to_all x1 -> x0, blocking collectives: 16.1 us -> none  [on_device(): lax.all_to_all(weight, 'rep', split_axis=1, concat_axis=0, tiled=True)]
    dot_general x6 -> x0, matrix products: 13.1 us -> none  [the longest x1 2.98 us: on_device(): lax.dot_general(aggregated, piece, (((1,), (1,)), ((), ())), preferred_el...]
  transfers between devices with their start and end apart: 5 -> 0, of which waited for: 5 -> 0; matrix products, arithmetic and copies ran while one was open for 1% -> 0% of each run, Pallas kernels for 0% -> 0%
where the time goes in v1:
time: 96.3 us; the launch traced here: 96.2 us
  Pallas kernels  95.5 us (99%)
    pallas_call x1, Pallas kernels, on_device(): pl.pallas_call(kernel, out_shape=outs, in_specs=[hbm] * 7, out_specs=(vm,...  86.5 us
    pallas_call x1, Pallas kernels, on_device(): pl.pallas_call(hand_over, out_shape=outs, in_specs=[hbm] * len(outs), out...  9.07 us

profile of v1, /device:TPU:1, one launch (start us, length us, event | category | flops | bytes accessed | tf_op | source)
XLA Modules:
  0.0 96.2 jit_solution(5795826068600662710)
XLA Ops:
  0.6 86.5 %graph_conv.1 = (bf16[32,1024]{1,0:T(8,128)(2,1)}, f32[32,1024]{1,0:T(8,128)}, bf16[32,1024]{1,0:T(8,128)(2,1)}) custom-call(bf16[32,1024]{1,0:T(8,128)(2,1)} %feat_hbm.1, bf16[64,128,128]{2,1,0:T(8,128)(2,1)} %tv_hbm.1, bf16[32,1024]{1,0:T(8,128)(2,1)} %w_hbm.1, bf16[32,1024]{1,0:T(8,128)(2,1)} %cot_hbm.1, s32[1,64]{1,0:T(1,128)} %bitcast.3, ...), custom_call_target="tpu_custom_call" | custom-call | tf_op jit(solution)/shard_map/graph_conv/pallas_call | solution.py:450
  87.1 9.1 %hand_over.1 = (bf16[32,1024]{1,0:T(8,128)(2,1)}, f32[32,1024]{1,0:T(8,128)}, bf16[32,1024]{1,0:T(8,128)(2,1)}) custom-call(bf16[32,1024]{1,0:T(8,128)(2,1)} %get-tuple-element.6.refs_0_, f32[32,1024]{1,0:T(8,128)} %get-tuple-element.7.refs_1_, bf16[32,1024]{1,0:T(8,128)(2,1)} %get-tuple-element.8.refs_2_), custom_call_target="tpu_custom_call" | custom-call | tf_op jit(solution)/shard_map/hand_over/pallas_call | solution.py:464

commit v2 on v1

--- a/solution.py
+++ b/solution.py
@@ -78,7 +78,7 @@
     )
     sems = dict(
         fz=1, fx0=x1, fx1=x1, fc0=X, fc1=X, w1=z1, w2=x1, w3=X, ct=z1, ag=z1, pp=y1, gp=y1, act=z1, ga=z1,
-        p=1, dx=x1, dz=z1, dt=1, ow=2 * X, d0=1, d1=1, e0=x1, e1=x1, gz=1,
+        p=1, dx=x1, dz=z1, dt=1, ow=2 * X, d0=1, d1=1, e0=2 * x1, e1=x1, gz=2,
     )
     smem = dict(itab=((8, nk), jnp.int32), ftab=((2 * bpd + 8, nk), F32))
     return bufs, sems, smem
@@ -229,10 +229,11 @@
         cp.wait()
     acc = tuple(ftab[2 * bpd, b] * dot(gown[me * bpd + b], tv[b], 1, 1) for b in range(bpd))
 
-    def forward(g, half, m, acc):
+    def forward(g, half, i, acc):
         acc = list(acc)
-        for j in range(PER):
-            k = (half * Q + m) * PER + j
+        for j in range(C * PER):
+            m = i * C + j // PER
+            k = (half * Q + i * C) * PER + j
             out = dot(g[m * bpd + itab[1, k]], tv[itab[0, k]], 1, 1)
             for b in range(bpd):
                 acc[b] = acc[b] + ftab[b, k] * out
@@ -244,7 +245,7 @@
     send(goth.at[mine], goth.at[mine], "fc1", 0, sib)
     for d in range(X):
         got(gown.at[seg(down(x, d, X) * C + co)], "fc0", d)
-    acc = lax.fori_loop(1, Q, lambda d, a: forward(gown, zh, lax.rem(me + d, Q), a), acc)
+    acc = lax.fori_loop(0, Q // C, lambda i, a: forward(gown, zh, i, a), acc)
     for d in range(1, X):
         part = goth.at[seg(down(x, d, X) * C + c)]
         got(part, "fx1", d - 1)
@@ -256,7 +257,7 @@
     send(wg.at[me], wg.at[me], "w3", 0, sib)
     for d in range(X):
         got(goth.at[seg(down(x, d, X) * C + co)], "fc1", d)
-    acc = lax.fori_loop(0, Q, lambda m, a: forward(goth, zo, m, a), acc)
+    acc = lax.fori_loop(0, Q // C, lambda i, a: forward(goth, zo, i, a), acc)
 
     A = B["A"]
     for b in range(bpd):
@@ -346,36 +347,46 @@
                 outs[b] = term if j == 0 else outs[b] + term
         return outs
 
-    def contribute(half, core, start, stop, at, into):
-        def step(i, carry):
-            i = at(i)
-            for b, out in enumerate(backward(half, i * C + core)):
-                into[i, b] = out.astype(into.dtype)
+    def contribute(half, core, into):
+        step = 2 if X % 2 == 0 else 1
+
+        def some(i, carry):
+            for n in range(step):
+                for b, out in enumerate(backward(half, (i * step + n) * C + core)):
+                    into[i * step + n, b] = out.astype(into.dtype)
             return carry
-        lax.fori_loop(start, stop, step, 0)
+        lax.fori_loop(0, X // step, some, 0)
 
     Dsib, Drec, Dkeep = (B["Dsib0"], B["Dsib1"]), (B["Drec0"], B["Drec1"]), (B["Dkeep0"], B["Dkeep1"])
     EXs, EXr = (B["EXs0"], B["EXs1"]), (B["EXr0"], B["EXr1"])
 
-    def to_x(n):
-        got(Drec[n], "d%d" % n, 0)
+    parts = 2 if bpd % 2 == 0 else 1
+
+    def cut(i):
+        return pl.ds(i * (bpd // parts), bpd // parts)
+
+    whole = pl.ds(0, bpd)
+
+    def to_x(n, at=whole, i=0):
         for d in range(1, X):
             x_ = up(x, d, X)
-            EXs[n][d - 1] = (Dkeep[n][x_] + Drec[n][x_].astype(F32)).astype(BF)
-            send(EXs[n].at[d - 1], EXr[n].at[d - 1], "e%d" % n, d - 1, dev(x_=x_))
-
-    def from_x(n):
-        total = Dkeep[n][x] + Drec[n][x].astype(F32)
+            EXs[n][d - 1, at] = (Dkeep[n][x_, at] + Drec[n][x_, at].astype(F32)).astype(BF)
+            send(EXs[n].at[d - 1, at], EXr[n].at[d - 1, at], "e%d" % n, i * (X - 1) + d - 1, dev(x_=x_))
+
+    def from_x(n, at=whole, i=0):
+        total = Dkeep[n][x, at] + Drec[n][x, at].astype(F32)
         for d in range(1, X):
-            got(EXr[n].at[d - 1], "e%d" % n, d - 1)
-            total = total + EXr[n][d - 1].astype(F32)
+            got(EXr[n].at[d - 1, at], "e%d" % n, i * (X - 1) + d - 1)
+            total = total + EXr[n][d - 1, at].astype(F32)
         return total
 
-    contribute(zo, co, 0, X, lambda i: i, Dsib[0])
+    contribute(zo, co, Dsib[0])
     send(Dsib[0], Drec[0], "d0", 0, sib)
-    contribute(zo, c, 0, X, lambda i: i, Dkeep[0])
-
-    to_x(0)
+    contribute(zo, c, Dkeep[0])
+
+    got(Drec[0], "d0", 0)
+    for i in range(parts):
+        to_x(0, cut(i), i)
     S32, Sb, DZr = B["S32"], B["Sb"], B["DZr"]
     total = PO[x] + PR[x].astype(F32)
     for d in range(1, X):
@@ -386,15 +397,11 @@
     for d in range(1, ZL):
         z = up(zl, d, ZL)
         send(Sb.at[z], DZr.at[d - 1], "dz", d - 1, dev(zl_=z))
-    contribute(zh, co, 0, X, lambda i: i, Dsib[1])
+    contribute(zh, co, Dsib[1])
     send(Dsib[1], Drec[1], "d1", 0, sib)
-    contribute(zh, c, 1, X, lambda i: lax.rem(x + i, X), Dkeep[1])
+    contribute(zh, c, Dkeep[1])
     for b in range(bpd):
         Dkeep[1][x, b] = ftab[2 * bpd, b] * dot(GA[b], tv[b], 1, 0)
-    FZs, FZr = B["FZs"], B["FZr"]
-    FZs[...] = from_x(0).astype(BF)
-    send(FZs, FZr, "gz", 0, anti)
-
     total = S32[zl]
     for d in range(1, ZL):
         got(DZr.at[d - 1], "dz", d - 1)
@@ -402,6 +409,12 @@
     Ts, Tr, OutW = B["Ts"], B["Tr"], B["OutW"]
     Ts[...] = total
     send(Ts, Tr, "dt", 0, anti)
+    FZs, FZr = B["FZs"], B["FZr"]
+    for i in range(parts):
+        at = cut(i)
+        FZs[at] = from_x(0, at, i).astype(BF)
+        send(FZs.at[at], FZr.at[at], "gz", i, anti)
+    got(Drec[1], "d1", 0)
     to_x(1)
     for d in range(1, ZL):
         got(actr.at[down(zl, d, ZL)], "act", d - 1)
@@ -418,22 +431,13 @@
         got(OutW.at[down(x, d, X) * C + (co if e else c)], "ow", n)
     for q in range(Q):
         gw_o[:, q * qw:(q + 1) * qw] = OutW[q]
-    got(FZr, "gz", 0)
+    for i in range(parts):
+        got(FZr.at[cut(i)], "gz", i)
     own = (own + FZr[...].astype(F32)).astype(BF)
     for b in range(bpd):
         gf_o[:, b * tb:(b + 1) * tb] = own[b]
     for cp in sent:
         cp.wait_send()
-
-
-def hand_over(*refs):
-    sem = refs[-1]
-    n = (len(refs) - 1) // 2
-    copies = [pltpu.make_async_copy(refs[i], refs[n + i], sem.at[i]) for i in range(n)]
-    for cp in copies:
-        cp.start()
-    for cp in copies:
-        cp.wait()
 
 
 def on_device(cfg, features_t, tile_dst, tile_src, tile_edges, tile_values, weight, cotangent):
@@ -443,11 +447,11 @@
     vm, hbm = pl.BlockSpec(memory_space=pltpu.VMEM), pl.BlockSpec(memory_space=pltpu.HBM)
     kernel = functools.partial(body, cfg, tuple(bufs), tuple(sems))
     outs = (
-        jax.ShapeDtypeStruct(features_t.shape, BF),
-        jax.ShapeDtypeStruct(weight.shape, F32),
-        jax.ShapeDtypeStruct(features_t.shape, BF),
+        pltpu.VMEM(features_t.shape, BF),
+        pltpu.VMEM(weight.shape, F32),
+        pltpu.VMEM(features_t.shape, BF),
     )
-    results = pl.pallas_call(
+    return pl.pallas_call(
         kernel,
         out_shape=outs,
         in_specs=[hbm] * 7,
@@ -457,19 +461,10 @@
         + [pltpu.SemaphoreType.DMA((9,))]
         + [pltpu.SMEM(s, t) for s, t in smem.values()],
         compiler_params=pltpu.CompilerParams(
-            collective_id=0, has_side_effects=True, vmem_limit_bytes=63 * 1024 * 1024
+            collective_id=0, has_side_effects=True, vmem_limit_bytes=62 * 1024 * 1024
         ),
         name="graph_conv",
     )(features_t, tile_values, weight, cotangent, *(v.reshape(1, nt) for v in (tile_dst, tile_src, tile_edges)))
-    return pl.pallas_call(
-        hand_over,
-        out_shape=outs,
-        in_specs=[hbm] * len(outs),
-        out_specs=(hbm,) * len(outs),
-        scratch_shapes=[pltpu.SemaphoreType.DMA((len(outs),))],
-        compiler_params=pltpu.CompilerParams(vmem_limit_bytes=63 * 1024 * 1024),
-        name="hand_over",
-    )(*results)
 
 
 def solution(mesh, cfg=None):

time: 96.3 us -> 86 us (0.89)
  Pallas kernels: 95.5 us -> 83.3 us
  local copies, waits for them, and re-layouts: 0 us -> 1.92 us
    pallas_call x1 -> x0, Pallas kernels: 9.07 us -> none  [on_device(): pl.pallas_call(hand_over, out_shape=outs, in_specs=[hbm] * len(outs), out...]
    pallas_call x1, Pallas kernels: 86.5 us -> 83.3 us  [on_device(): pl.pallas_call(kernel, out_shape=outs, in_specs=[hbm] * 7, out_specs=(vm,...]
    unnamed x0 -> x3, local copies, waits for them, and re-layouts: none -> 1.92 us
where the time goes in v2:
time: 86 us; the launch traced here: 85.9 us
  Pallas kernels  83.3 us (97%)
  local copies, waits for them, and re-layouts  1.92 us (2%)
    pallas_call x1, Pallas kernels, on_device(): pl.pallas_call(kernel, out_shape=outs, in_specs=[hbm] * 7, out_specs=(vm,...  83.3 us
    unnamed x3, local copies, waits for them, and re-layouts  1.92 us

profile of v2, /device:TPU:1, one launch (start us, length us, event | category | flops | bytes accessed | tf_op | source)
XLA Modules:
  0.0 85.9 jit_solution(12963939711018229427)
XLA Ops:
  0.6 83.3 %graph_conv.1 = (bf16[32,1024]{1,0:T(8,128)(2,1)S(1)}, f32[32,1024]{1,0:T(8,128)S(1)}, bf16[32,1024]{1,0:T(8,128)(2,1)S(1)}) custom-call(bf16[32,1024]{1,0:T(8,128)(2,1)} %feat_hbm.1, bf16[64,128,128]{2,1,0:T(8,128)(2,1)} %tv_hbm.1, bf16[32,1024]{1,0:T(8,128)(2,1)} %w_hbm.1, bf16[32,1024]{1,0:T(8,128)(2,1)} %cot_hbm.1, s32[1,64]{1,0:T(1,128)} %bitcast.3, ...), custom_call_target="tpu_custom_call" | custom-call | tf_op jit(solution)/shard_map/graph_conv/pallas_call | solution.py:454
  84.0 0.6 copy.13
  84.6 0.6 copy.15
  85.2 0.7 copy.14

commit v3 on v2

--- a/solution.py
+++ b/solution.py
@@ -23,7 +23,6 @@
     Q = X * C
     F = rb * Y * ZL
     qw = F // Q
-    qy = Q // Y
     bpd = ZL
     x1, y1, z1 = max(X - 1, 1), max(Y - 1, 1), max(ZL - 1, 1)
     nk = -(-cfg["ZH"] * Q * PER // 128) * 128
@@ -40,14 +39,15 @@
         goth=((Q * bpd, rb, tb), BF),
         tv=((nt, tb, tb), BF),
         wb=((Q, rb, qw), BF),
-        wg=((Q, ZL, rb, qw), BF),
+        wg=((Y, C, X, ZL, rb, qw), BF),
         cb=((bpd, rb, tb), BF),
         ct=((ZL, rb, tb), BF),
         aggb=((bpd, rb, tb), BF),
         A=((ZL, rb, tb), BF),
-        pps=((y1, qy, qw, tb), BF),
-        ppr=((y1, qy, qw, tb), BF),
-        GP=((Q, qw, tb), BF),
+        ctT=((Y, tb, rb * ZL), BF),
+        AT=((Y, tb, rb * ZL), BF),
+        preT=((X, tb, C * qw), F32),
+        gpT=((Q, tb, qw), BF),
         actb=((ZL, rb, tb), BF),
         actr=((bpd, rb, tb), BF),
         gab=((ZL, rb, tb), BF),
@@ -77,7 +77,7 @@
         FZr=((bpd, rb, tb), BF),
     )
     sems = dict(
-        fz=1, fx0=x1, fx1=x1, fc0=X, fc1=X, w1=z1, w2=x1, w3=X, ct=z1, ag=z1, pp=y1, gp=y1, act=z1, ga=z1,
+        fz=1, fx0=x1, fx1=x1, fc0=X, fc1=X, w1=z1, w2=x1, w3=Y, w4=2, w5=2, ct=z1, cty=y1, ag=z1, agy=y1, act=z1, ga=z1,
         p=1, dx=x1, dz=z1, dt=1, ow=2 * X, d0=1, d1=1, e0=2 * x1, e1=x1, gz=2,
     )
     smem = dict(itab=((8, nk), jnp.int32), ftab=((2 * bpd + 8, nk), F32))
@@ -131,7 +131,6 @@
     bpd = ZL
     rb, tb = B["A"].shape[1:]
     qw = B["wb"].shape[2]
-    qy = Q // Y
     rows = ZL * rb
 
     blk, rep = lax.axis_index("blk"), lax.axis_index("rep")
@@ -214,12 +213,12 @@
         B["cb"][b] = cot[:, b * tb:(b + 1) * tb]
     for q in range(Q):
         B["wb"][q] = w[:, q * qw:(q + 1) * qw]
-    B["wg"][me, zl] = B["wb"][me]
+    B["wg"][y, c, x, zl] = B["wb"][me]
     B["ct"][zl] = B["cb"][zl]
     wg, wb = B["wg"], B["wb"]
     for d in range(1, ZL):
         z = up(zl, d, ZL)
-        send(wb.at[me], wg.at[me, zl], "w1", d - 1, dev(zl_=z))
+        send(wb.at[me], wg.at[y, c, x, zl], "w1", d - 1, dev(zl_=z))
     for d in range(1, X):
         part = gown.at[seg(down(x, d, X) * C + c)]
         got(part, "fx0", d - 1)
@@ -239,22 +238,37 @@
                 acc[b] = acc[b] + ftab[b, k] * out
         return tuple(acc)
 
+    for d in range(1, ZL):
+        got(wg.at[y, c, x, down(zl, d, ZL)], "w1", d - 1)
+    for d in range(1, X):
+        send(wg.at[y, c, x], wg.at[y, c, x], "w2", d - 1, dev(x_=up(x, d, X)))
     got(goth.at[mine], "fz", 0)
     for d in range(1, X):
         send(goth.at[mine], goth.at[mine], "fx1", d - 1, dev(x_=up(x, d, X)))
     send(goth.at[mine], goth.at[mine], "fc1", 0, sib)
+    for d in range(1, ZL):
+        z = up(zl, d, ZL)
+        send(B["cb"].at[z], B["ct"].at[zl], "ct", d - 1, dev(zl_=z))
     for d in range(X):
         got(gown.at[seg(down(x, d, X) * C + co)], "fc0", d)
     acc = lax.fori_loop(0, Q // C, lambda i, a: forward(gown, zh, i, a), acc)
     for d in range(1, X):
+        got(wg.at[y, c, down(x, d, X)], "w2", d - 1)
+    y_up, y_down, y_far = up(y, 1, Y), down(y, 1, Y), up(y, 2, Y)
+    send(wg.at[y, c], wg.at[y, c], "w4", 0, dev(y_=y_up))
+    if Y > 2:
+        send(wg.at[y, c], wg.at[y, c], "w4", 1, dev(y_=y_down))
+    send(wg.at[y, c], wg.at[y, c], "w3", 0, sib)
+    for d in range(1, X):
         part = goth.at[seg(down(x, d, X) * C + c)]
         got(part, "fx1", d - 1)
         send(part, part, "fc1", d, sib)
     for d in range(1, ZL):
-        got(wg.at[me, down(zl, d, ZL)], "w1", d - 1)
-    for d in range(1, X):
-        send(wg.at[me], wg.at[me], "w2", d - 1, dev(x_=up(x, d, X)))
-    send(wg.at[me], wg.at[me], "w3", 0, sib)
+        got(B["ct"].at[down(zl, d, ZL)], "ct", d - 1)
+    ctT, AT = B["ctT"], B["AT"]
+    ctT[y] = B["ct"][...].reshape(rows, tb).astype(F32).T.astype(BF)
+    for d in range(1, Y):
+        send(ctT.at[y], ctT.at[y], "cty", d - 1, dev(y_=up(y, d, Y)))
     for d in range(X):
         got(goth.at[seg(down(x, d, X) * C + co)], "fc1", d)
     acc = lax.fori_loop(0, Q // C, lambda i, a: forward(goth, zo, i, a), acc)
@@ -266,55 +280,57 @@
     for d in range(1, ZL):
         z = up(zl, d, ZL)
         send(B["aggb"].at[z], A.at[zl], "ag", d - 1, dev(zl_=z))
-    for d in range(1, ZL):
-        z = up(zl, d, ZL)
-        send(B["cb"].at[z], B["ct"].at[zl], "ct", d - 1, dev(zl_=z))
-    for d in range(1, X):
-        part = wg.at[down(x, d, X) * C + c]
-        got(part, "w2", d - 1)
-        send(part, part, "w3", d, sib)
-    for d in range(X):
-        got(wg.at[down(x, d, X) * C + co], "w3", d)
+    half = X // 2
+    got(wg.at[y_down, c], "w4", 0)
+    send(wg.at[y_down, c], wg.at[y_down, c], "w3", 1, sib)
+    if Y > 2:
+        part = wg.at[y_down, c, pl.ds(0, half)]
+        send(part, part, "w5", 0, dev(y_=y_up))
+        got(wg.at[y_up, c], "w4", 1)
+        send(wg.at[y_up, c], wg.at[y_up, c], "w3", 2, sib)
+        part = wg.at[y_up, c, pl.ds(half, half)]
+        send(part, part, "w5", 1, dev(y_=y_down))
     for d in range(1, ZL):
         got(A.at[down(zl, d, ZL)], "ag", d - 1)
 
     a2 = A[...].reshape(rows, tb)
-
-    def pre_part(y_, i):
-        return dot(wg[y_ * qy + i].reshape(rows, qw), a2, 0, 0)
-
-    pps, ppr, GP = B["pps"], B["ppr"], B["GP"]
+    AT[y] = a2.astype(F32).T.astype(BF)
     for d in range(1, Y):
-        y_ = up(y, d, Y)
-        for i in range(qy):
-            pps[d - 1, i] = pre_part(y_, i).astype(BF)
-        send(pps.at[d - 1], ppr.at[d - 1], "pp", d - 1, dev(y_=y_))
-    pre = jnp.concatenate([pre_part(y, i) for i in range(qy)], axis=0)
-    for d in range(1, ZL):
-        got(B["ct"].at[down(zl, d, ZL)], "ct", d - 1)
-    cotangent = B["ct"][...].reshape(rows, tb).astype(F32)
+        send(AT.at[y], AT.at[y], "agy", d - 1, dev(y_=up(y, d, Y)))
+
+    def weight_of(y_, i):
+        return jnp.concatenate([wg[y_, e, i].reshape(rows, qw) for e in range(C)], axis=1)
+
+    preT, gpT = B["preT"], B["gpT"]
+    got(wg.at[y, co], "w3", 0)
+    for i in range(X):
+        preT[i] = dot(AT[y], weight_of(y, i), 1, 0)
+    if Y > 2:
+        got(wg.at[y_far, c, pl.ds(0, half)], "w5", 0)
+        got(wg.at[y_far, c, pl.ds(half, half)], "w5", 1)
+        send(wg.at[y_far, c], wg.at[y_far, c], "w3", 3, sib)
     for d in range(1, Y):
-        got(ppr.at[d - 1], "pp", d - 1)
-        pre = pre + ppr[d - 1].reshape(rows, tb).astype(F32)
-    sig = jax.nn.sigmoid(pre)
-    gp = (cotangent * sig * (1.0 + pre * (1.0 - sig))).astype(BF).reshape(qy, qw, tb)
-    for i in range(qy):
-        GP[y * qy + i] = gp[i]
-    for d in range(1, Y):
-        part = GP.at[pl.ds(y * qy, qy)]
-        send(part, part, "gp", d - 1, dev(y_=up(y, d, Y)))
-    actb, actr = B["actb"], B["actr"]
-    actb[...] = (pre * sig).astype(BF).reshape(ZL, rb, tb)
-    actr[zl] = actb[zl]
-    for d in range(1, ZL):
-        z = up(zl, d, ZL)
-        send(actb.at[z], actr.at[zl], "act", d - 1, dev(zl_=z))
-    for d in range(1, Y):
-        got(GP.at[pl.ds(down(y, d, Y) * qy, qy)], "gp", d - 1)
-
-    ga = dot(wg[0].reshape(rows, qw), GP[0], 1, 0)
-    for q in range(1, Q):
-        ga = ga + dot(wg[q].reshape(rows, qw), GP[q], 1, 0)
+        got(ctT.at[down(y, d, Y)], "cty", d - 1)
+    order = [(1, 1), (3, 2), (2, 3)] if Y > 2 else [(1, 1)]
+    for n, (d, at) in enumerate(order):
+        y_ = down(y, d, Y)
+        got(wg.at[y_, co], "w3", at)
+        got(AT.at[y_], "agy", d - 1)
+        for i in range(X):
+            pre = preT[i] + dot(AT[y_], weight_of(y_, i), 1, 0)
+            preT[i] = pre
+            if n == len(order) - 1:
+                sig = jax.nn.sigmoid(pre)
+                gp = (ctT[i].astype(F32) * sig * (1.0 + pre * (1.0 - sig))).astype(BF)
+                for e in range(C):
+                    gpT[i * C + e] = gp[:, e * qw:(e + 1) * qw]
+
+    def grad_pre(i):
+        return jnp.concatenate([gpT[i * C + e] for e in range(C)], axis=1)
+
+    ga = dot(weight_of(y, 0), grad_pre(0), 1, 1)
+    for i in range(1, X):
+        ga = ga + dot(weight_of(y, i), grad_pre(i), 1, 1)
     gab, GA = B["gab"], B["GA"]
     gab[...] = ga.astype(BF).reshape(ZL, rb, tb)
     GA[zl] = gab[zl]
@@ -324,10 +340,10 @@
 
     PS, PO, PR = B["PS"], B["PO"], B["PR"]
     for i in range(X):
-        PS[i] = dot(a2, GP[i * C + co], 1, 1).astype(BF).reshape(ZL, rb, qw)
+        PS[i] = dot(a2, gpT[i * C + co], 1, 0).astype(BF).reshape(ZL, rb, qw)
     send(PS, PR, "p", 0, sib)
     for i in range(X):
-        PO[i] = dot(a2, GP[i * C + c], 1, 1).reshape(ZL, rb, qw)
+        PO[i] = dot(a2, gpT[i * C + c], 1, 0).reshape(ZL, rb, qw)
     got(PR, "p", 0)
     DXs, DXr = B["DXs"], B["DXr"]
     for d in range(1, X):
@@ -399,6 +415,13 @@
         send(Sb.at[z], DZr.at[d - 1], "dz", d - 1, dev(zl_=z))
     contribute(zh, co, Dsib[1])
     send(Dsib[1], Drec[1], "d1", 0, sib)
+    actb, actr = B["actb"], B["actr"]
+    pre = preT[y]
+    actb[...] = (pre * jax.nn.sigmoid(pre)).T.astype(BF).reshape(ZL, rb, tb)
+    actr[zl] = actb[zl]
+    for d in range(1, ZL):
+        z = up(zl, d, ZL)
+        send(actb.at[z], actr.at[zl], "act", d - 1, dev(zl_=z))
     contribute(zh, c, Dkeep[1])
     for b in range(bpd):
         Dkeep[1][x, b] = ftab[2 * bpd, b] * dot(GA[b], tv[b], 1, 0)

time: 86 us -> 80.5 us (0.936); the launches traced: 85.9 us -> 79 us
  Pallas kernels: 83.3 us -> 76.5 us
    pallas_call x1, Pallas kernels: 83.3 us -> 76.5 us  [on_device(): pl.pallas_call(kernel, out_shape=outs, in_specs=[hbm] * 7, out_specs=(vm,...]
where the time goes in v3:
time: 80.5 us; the launch traced here: 79 us
  Pallas kernels  76.5 us (95%)
  local copies, waits for them, and re-layouts  1.92 us (2%)
    pallas_call x1, Pallas kernels, on_device(): pl.pallas_call(kernel, out_shape=outs, in_specs=[hbm] * 7, out_specs=(vm,...  76.5 us
    unnamed x3, local copies, waits for them, and re-layouts  1.92 us

profile of v3, /device:TPU:1, one launch (start us, length us, event | category | flops | bytes accessed | tf_op | source)
XLA Modules:
  0.0 79.0 jit_solution(9132803040056566500)
XLA Ops:
  0.6 76.5 %graph_conv.1 = (bf16[32,1024]{1,0:T(8,128)(2,1)S(1)}, f32[32,1024]{1,0:T(8,128)S(1)}, bf16[32,1024]{1,0:T(8,128)(2,1)S(1)}) custom-call(bf16[32,1024]{1,0:T(8,128)(2,1)} %feat_hbm.1, bf16[64,128,128]{2,1,0:T(8,128)(2,1)} %tv_hbm.1, bf16[32,1024]{1,0:T(8,128)(2,1)} %w_hbm.1, bf16[32,1024]{1,0:T(8,128)(2,1)} %cot_hbm.1, s32[1,64]{1,0:T(1,128)} %bitcast.3, ...), custom_call_target="tpu_custom_call" | custom-call | tf_op jit(solution)/shard_map/graph_conv/pallas_call | solution.py:477
  77.1 0.6 copy.13
  77.8 0.6 copy.15
  78.4 0.7 copy.14

commit v4 on v3

--- a/solution.py
+++ b/solution.py
@@ -16,6 +16,10 @@
 
 def dot(a, b, ca, cb):
     return lax.dot_general(a, b, (((ca,), (cb,)), ((), ())), preferred_element_type=F32)
+
+
+def groups(n):
+    return 2 if n % 2 == 0 else 1
 
 
 def shapes(cfg, rb, tb, nt):
@@ -35,6 +39,8 @@
         ev=((1, nt), jnp.int32),
         itv=((8, nk), jnp.int32),
         ftv=((2 * bpd + 8, nk), F32),
+        ZR=((bpd // groups(bpd), rb, tb), BF),
+        FR=((bpd // groups(bpd), rb, tb), BF),
         gown=((Q * bpd, rb, tb), BF),
         goth=((Q * bpd, rb, tb), BF),
         tv=((nt, tb, tb), BF),
@@ -45,7 +51,7 @@
         aggb=((bpd, rb, tb), BF),
         A=((ZL, rb, tb), BF),
         ctT=((Y, tb, rb * ZL), BF),
-        AT=((Y, tb, rb * ZL), BF),
+        AT=((Y, groups(ZL), tb, rb * ZL // groups(ZL)), BF),
         preT=((X, tb, C * qw), F32),
         gpT=((Q, tb, qw), BF),
         actb=((ZL, rb, tb), BF),
@@ -77,8 +83,8 @@
         FZr=((bpd, rb, tb), BF),
     )
     sems = dict(
-        fz=1, fx0=x1, fx1=x1, fc0=X, fc1=X, w1=z1, w2=x1, w3=Y, w4=2, w5=2, ct=z1, cty=y1, ag=z1, agy=y1, act=z1, ga=z1,
-        p=1, dx=x1, dz=z1, dt=1, ow=2 * X, d0=1, d1=1, e0=2 * x1, e1=x1, gz=2,
+        zr=1, fz=2, fx0=x1, fx1=2 * x1, fc0=X, fc1=2 * X, w1=z1, w2=x1, w3=Y, w4=2, w5=2, ct=z1, cty=y1, ag=z1, agy=2 * y1, act=z1, ga=z1,
+        p=1, dx=x1, dz=z1, dt=1, ow=2 * X, d0=1, d1=1, e0=2 * x1, e1=x1, fr=1, gz=2,
     )
     smem = dict(itab=((8, nk), jnp.int32), ftab=((2 * bpd + 8, nk), F32))
     return bufs, sems, smem
@@ -150,6 +156,14 @@
         return lax.rem(v + n - d, n)
 
     anti, sib = dev(zh_=zo), dev(c_=co)
+    nz = ZH * ZL
+
+    def dev_z(d):
+        z_ = lax.rem(zh * ZL + zl + d + nz, nz)
+        return dev(zh_=lax.div(z_, ZL), zl_=lax.rem(z_, ZL))
+
+    parts = groups(bpd)
+    size = bpd // parts
     sent = []
 
     def send(src, dst, name, i, to):
@@ -177,7 +191,7 @@
         ld.start()
 
     barrier = pltpu.get_barrier_semaphore()
-    partners = [anti]
+    partners = [anti, *(dev_z(d) for d in (1, -1, ZL - 1, 1 - ZL))]
     partners += [dev(x_=up(x, d, X), c_=(c if e == 0 else co)) for d in range(X) for e in range(C) if d or e]
     partners += [dev(zl_=up(zl, d, ZL)) for d in range(1, ZL)]
     partners += [dev(y_=up(y, d, Y)) for d in range(1, Y)]
@@ -193,13 +207,22 @@
     def seg(m):
         return pl.ds(m * bpd, bpd)
 
+    def sub(m, i):
+        return pl.ds(m * bpd + i * size, size)
+
     mine = seg(me)
-    send(gown.at[mine], goth.at[mine], "fz", 0, anti)
+    if parts > 1:
+        send(gown.at[sub(me, 0)], B["ZR"], "zr", 0, dev_z(-1))
+    last = sub(me, parts - 1)
+    send(gown.at[last], goth.at[last], "fz", parts - 1, anti)
     for d in range(1, X):
         send(gown.at[mine], gown.at[mine], "fx0", d - 1, dev(x_=up(x, d, X)))
     send(gown.at[mine], gown.at[mine], "fc0", 0, sib)
     for ld in loads[4:]:
         ld.wait()
+    if parts > 1:
+        got(B["ZR"], "zr", 0)
+        send(B["ZR"], goth.at[sub(me, 0)], "fz", 0, dev_z(1 - ZL))
     tables(bpd, B["dv"][...], B["sv"][...], B["ev"][...], B["itv"], B["ftv"])
     to_smem = [
         pltpu.make_async_copy(B["itv"], itab, load_sem.at[7]),
@@ -242,10 +265,12 @@
         got(wg.at[y, c, x, down(zl, d, ZL)], "w1", d - 1)
     for d in range(1, X):
         send(wg.at[y, c, x], wg.at[y, c, x], "w2", d - 1, dev(x_=up(x, d, X)))
-    got(goth.at[mine], "fz", 0)
-    for d in range(1, X):
-        send(goth.at[mine], goth.at[mine], "fx1", d - 1, dev(x_=up(x, d, X)))
-    send(goth.at[mine], goth.at[mine], "fc1", 0, sib)
+    for i in reversed(range(parts)):
+        part = goth.at[sub(me, i)]
+        got(part, "fz", i)
+        for d in range(1, X):
+            send(part, part, "fx1", i * (X - 1) + d - 1, dev(x_=up(x, d, X)))
+        send(part, part, "fc1", i * X, sib)
     for d in range(1, ZL):
         z = up(zl, d, ZL)
         send(B["cb"].at[z], B["ct"].at[zl], "ct", d - 1, dev(zl_=z))
@@ -259,18 +284,20 @@
     if Y > 2:
         send(wg.at[y, c], wg.at[y, c], "w4", 1, dev(y_=y_down))
     send(wg.at[y, c], wg.at[y, c], "w3", 0, sib)
-    for d in range(1, X):
-        part = goth.at[seg(down(x, d, X) * C + c)]
-        got(part, "fx1", d - 1)
-        send(part, part, "fc1", d, sib)
+    for i in reversed(range(parts)):
+        for d in range(1, X):
+            part = goth.at[sub(down(x, d, X) * C + c, i)]
+            got(part, "fx1", i * (X - 1) + d - 1)
+            send(part, part, "fc1", i * X + d, sib)
     for d in range(1, ZL):
         got(B["ct"].at[down(zl, d, ZL)], "ct", d - 1)
     ctT, AT = B["ctT"], B["AT"]
     ctT[y] = B["ct"][...].reshape(rows, tb).astype(F32).T.astype(BF)
     for d in range(1, Y):
         send(ctT.at[y], ctT.at[y], "cty", d - 1, dev(y_=up(y, d, Y)))
-    for d in range(X):
-        got(goth.at[seg(down(x, d, X) * C + co)], "fc1", d)
+    for i in range(parts):
+        for d in range(X):
+            got(goth.at[sub(down(x, d, X) * C + co, i)], "fc1", i * X + d)
     acc = lax.fori_loop(0, Q // C, lambda i, a: forward(goth, zo, i, a), acc)
 
     A = B["A"]
@@ -290,13 +317,24 @@
         send(wg.at[y_up, c], wg.at[y_up, c], "w3", 2, sib)
         part = wg.at[y_up, c, pl.ds(half, half)]
         send(part, part, "w5", 1, dev(y_=y_down))
-    for d in range(1, ZL):
-        got(A.at[down(zl, d, ZL)], "ag", d - 1)
-
+    ng = groups(ZL)
+    hz = ZL // ng
+    near = lax.div(zl, hz)
+    for n in range(ng):
+        g = near if n == 0 else 1 - near
+        for e in range(hz):
+            if n == 0 and e == 0:
+                continue
+            from_z = g * hz + (lax.rem(zl - g * hz + e, hz) if n == 0 else e)
+            got(A.at[from_z], "ag", lax.rem(zl - from_z + ZL, ZL) - 1)
+        AT[y, g] = A[pl.ds(g * hz, hz)].reshape(rows // ng, tb).astype(F32).T.astype(BF)
+        for d in range(1, Y):
+            send(AT.at[y, g], AT.at[y, g], "agy", n * (Y - 1) + d - 1, dev(y_=up(y, d, Y)))
     a2 = A[...].reshape(rows, tb)
-    AT[y] = a2.astype(F32).T.astype(BF)
-    for d in range(1, Y):
-        send(AT.at[y], AT.at[y], "agy", d - 1, dev(y_=up(y, d, Y)))
+
+    def nodes_by_rows(y_):
+        return jnp.concatenate([AT[y_, g] for g in range(ng)], axis=1)
+
 
     def weight_of(y_, i):
         return jnp.concatenate([wg[y_, e, i].reshape(rows, qw) for e in range(C)], axis=1)
@@ -304,7 +342,7 @@
     preT, gpT = B["preT"], B["gpT"]
     got(wg.at[y, co], "w3", 0)
     for i in range(X):
-        preT[i] = dot(AT[y], weight_of(y, i), 1, 0)
+        preT[i] = dot(nodes_by_rows(y), weight_of(y, i), 1, 0)
     if Y > 2:
         got(wg.at[y_far, c, pl.ds(0, half)], "w5", 0)
         got(wg.at[y_far, c, pl.ds(half, half)], "w5", 1)
@@ -315,9 +353,10 @@
     for n, (d, at) in enumerate(order):
         y_ = down(y, d, Y)
         got(wg.at[y_, co], "w3", at)
-        got(AT.at[y_], "agy", d - 1)
+        for g in range(ng):
+            got(AT.at[y_, near if g == 0 else 1 - near], "agy", g * (Y - 1) + d - 1)
         for i in range(X):
-            pre = preT[i] + dot(AT[y_], weight_of(y_, i), 1, 0)
+            pre = preT[i] + dot(nodes_by_rows(y_), weight_of(y_, i), 1, 0)
             preT[i] = pre
             if n == len(order) - 1:
                 sig = jax.nn.sigmoid(pre)
@@ -376,10 +415,8 @@
     Dsib, Drec, Dkeep = (B["Dsib0"], B["Dsib1"]), (B["Drec0"], B["Drec1"]), (B["Dkeep0"], B["Dkeep1"])
     EXs, EXr = (B["EXs0"], B["EXs1"]), (B["EXr0"], B["EXr1"])
 
-    parts = 2 if bpd % 2 == 0 else 1
-
     def cut(i):
-        return pl.ds(i * (bpd // parts), bpd // parts)
+        return pl.ds(i * size, size)
 
     whole = pl.ds(0, bpd)
 
@@ -436,7 +473,13 @@
     for i in range(parts):
         at = cut(i)
         FZs[at] = from_x(0, at, i).astype(BF)
-        send(FZs.at[at], FZr.at[at], "gz", i, anti)
+        if i < parts - 1:
+            send(FZs.at[at], B["FR"], "fr", 0, dev_z(-1))
+        else:
+            send(FZs.at[at], FZr.at[at], "gz", i, anti)
+    if parts > 1:
+        got(B["FR"], "fr", 0)
+        send(B["FR"], FZr.at[cut(0)], "gz", 0, dev_z(1 - ZL))
     got(Drec[1], "d1", 0)
     to_x(1)
     for d in range(1, ZL):

time: 80.5 us -> 86.7 us (1.077); the launches traced: 79 us -> 86.5 us
  Pallas kernels: 76.5 us -> 84 us
    pallas_call x1, Pallas kernels: 76.5 us -> 84 us  [on_device(): pl.pallas_call(kernel, out_shape=outs, in_specs=[hbm] * 7, out_specs=(vm,...]
where the time goes in v4:
time: 86.7 us; the launch traced here: 86.5 us
  Pallas kernels  84 us (97%)
  local copies, waits for them, and re-layouts  1.92 us (2%)
    pallas_call x1, Pallas kernels, on_device(): pl.pallas_call(kernel, out_shape=outs, in_specs=[hbm] * 7, out_specs=(vm,...  84 us
    unnamed x3, local copies, waits for them, and re-layouts  1.92 us

profile of v4, /device:TPU:1, one launch (start us, length us, event | category | flops | bytes accessed | tf_op | source)
XLA Modules:
  0.0 86.5 jit_solution(18110238511472540292)
XLA Ops:
  0.6 84.0 %graph_conv.1 = (bf16[32,1024]{1,0:T(8,128)(2,1)S(1)}, f32[32,1024]{1,0:T(8,128)S(1)}, bf16[32,1024]{1,0:T(8,128)(2,1)S(1)}) custom-call(bf16[32,1024]{1,0:T(8,128)(2,1)} %feat_hbm.1, bf16[64,128,128]{2,1,0:T(8,128)(2,1)} %tv_hbm.1, bf16[32,1024]{1,0:T(8,128)(2,1)} %w_hbm.1, bf16[32,1024]{1,0:T(8,128)(2,1)} %cot_hbm.1, s32[1,64]{1,0:T(1,128)} %bitcast.3, ...), custom_call_target="tpu_custom_call" | custom-call | tf_op jit(solution)/shard_map/graph_conv/pallas_call | solution.py:520
  84.6 0.6 copy.13
  85.3 0.6 copy.15
  85.9 0.7 copy.14

commit v5 on v3

--- a/solution.py
+++ b/solution.py
@@ -24,7 +24,7 @@
     F = rb * Y * ZL
     qw = F // Q
     bpd = ZL
-    x1, y1, z1 = max(X - 1, 1), max(Y - 1, 1), max(ZL - 1, 1)
+    x1, y1 = max(X - 1, 1), max(Y - 1, 1)
     nk = -(-cfg["ZH"] * Q * PER // 128) * 128
     bufs = dict(
         fv=((rb, bpd * tb), BF),
@@ -35,21 +35,21 @@
         ev=((1, nt), jnp.int32),
         itv=((8, nk), jnp.int32),
         ftv=((2 * bpd + 8, nk), F32),
-        gown=((Q * bpd, rb, tb), BF),
-        goth=((Q * bpd, rb, tb), BF),
+        gown=((X, C, bpd, rb, tb), BF),
+        goth=((X, C, bpd, rb, tb), BF),
         tv=((nt, tb, tb), BF),
+        CWs=((ZL, 2, rb, qw), BF),
+        CWr=((ZL, 2, rb, qw), BF),
         wb=((Q, rb, qw), BF),
         wg=((Y, C, X, ZL, rb, qw), BF),
-        cb=((bpd, rb, tb), BF),
-        ct=((ZL, rb, tb), BF),
         aggb=((bpd, rb, tb), BF),
         A=((ZL, rb, tb), BF),
         ctT=((Y, tb, rb * ZL), BF),
         AT=((Y, tb, rb * ZL), BF),
         preT=((X, tb, C * qw), F32),
         gpT=((Q, tb, qw), BF),
-        actb=((ZL, rb, tb), BF),
-        actr=((bpd, rb, tb), BF),
+        ADs=((ZL, 2, rb, tb), BF),
+        ADr=((ZL, 2, rb, tb), BF),
         gab=((ZL, rb, tb), BF),
         GA=((bpd, rb, tb), BF),
         PS=((X, ZL, rb, qw), BF),
@@ -57,9 +57,7 @@
         PR=((X, ZL, rb, qw), BF),
         DXs=((x1, ZL, rb, qw), BF),
         DXr=((x1, ZL, rb, qw), BF),
-        Sb=((ZL, rb, qw), BF),
         S32=((ZL, rb, qw), F32),
-        DZr=((z1, rb, qw), BF),
         Ts=((rb, qw), F32),
         Tr=((rb, qw), F32),
         OutW=((Q, rb, qw), F32),
@@ -77,8 +75,8 @@
         FZr=((bpd, rb, tb), BF),
     )
     sems = dict(
-        fz=1, fx0=x1, fx1=x1, fc0=X, fc1=X, w1=z1, w2=x1, w3=Y, w4=2, w5=2, ct=z1, cty=y1, ag=z1, agy=y1, act=z1, ga=z1,
-        p=1, dx=x1, dz=z1, dt=1, ow=2 * X, d0=1, d1=1, e0=2 * x1, e1=x1, gz=2,
+        fz=1, fx0=1, fx1=x1, fc0=1, fc1=1, cw=1, w2=1, w3=Y, w4=2, w5=2, cty=1, ag=1, agy=y1, ga=1,
+        p=1, dx=1, ad=1, dt=1, ow=1, d0=1, d1=1, e0=2, e1=1, gz=2,
     )
     smem = dict(itab=((8, nk), jnp.int32), ftab=((2 * bpd + 8, nk), F32))
     return bufs, sems, smem
@@ -152,19 +150,25 @@
     anti, sib = dev(zh_=zo), dev(c_=co)
     sent = []
 
-    def send(src, dst, name, i, to):
-        cp = pltpu.make_async_remote_copy(
+    def copy(src, dst, name, i, to):
+        return pltpu.make_async_remote_copy(
             src_ref=src, dst_ref=dst, send_sem=SS[name].at[i], recv_sem=RS[name].at[i],
             device_id=to, device_id_type=MESH,
         )
+
+    def send(src, dst, name, i, to):
+        cp = copy(src, dst, name, i, to)
         cp.start()
         sent.append(cp)
 
+    def send_all(copies, size_ref, name, i=0):
+        for src, dst, to in copies:
+            copy(src, dst, name, i, to).start()
+        if copies:
+            sent.append(copy(size_ref, size_ref, name, i, sib))
+
     def got(dst, name, i):
-        pltpu.make_async_remote_copy(
-            src_ref=dst, dst_ref=dst, send_sem=SS[name].at[i], recv_sem=RS[name].at[i],
-            device_id=sib, device_id_type=MESH,
-        ).wait_recv()
+        copy(dst, dst, name, i, sib).wait_recv()
 
     loads = [
         pltpu.make_async_copy(a, b, load_sem.at[i])
@@ -187,17 +191,13 @@
     gown, goth, tv = B["gown"], B["goth"], B["tv"]
     loads[0].wait()
     for b in range(bpd):
-        gown[me * bpd + b] = feat[:, b * tb:(b + 1) * tb]
+        gown[x, c, b] = feat[:, b * tb:(b + 1) * tb]
     pl.semaphore_wait(barrier, len(partners))
 
-    def seg(m):
-        return pl.ds(m * bpd, bpd)
-
-    mine = seg(me)
-    send(gown.at[mine], goth.at[mine], "fz", 0, anti)
-    for d in range(1, X):
-        send(gown.at[mine], gown.at[mine], "fx0", d - 1, dev(x_=up(x, d, X)))
-    send(gown.at[mine], gown.at[mine], "fc0", 0, sib)
+    xs = [up(x, d, X) for d in range(1, X)]
+    zs = [up(zl, d, ZL) for d in range(1, ZL)]
+    send(gown.at[x, c], goth.at[x, c], "fz", 0, anti)
+    send_all([(gown.at[x, c], gown.at[x, c], dev(x_=v)) for v in xs], gown.at[pl.ds(0, X - 1), 0], "fx0")
     for ld in loads[4:]:
         ld.wait()
     tables(bpd, B["dv"][...], B["sv"][...], B["ev"][...], B["itv"], B["ftv"])
@@ -209,77 +209,79 @@
         cp.start()
     loads[1].wait()
     loads[2].wait()
-    for b in range(bpd):
-        B["cb"][b] = cot[:, b * tb:(b + 1) * tb]
     for q in range(Q):
         B["wb"][q] = w[:, q * qw:(q + 1) * qw]
-    B["wg"][y, c, x, zl] = B["wb"][me]
-    B["ct"][zl] = B["cb"][zl]
-    wg, wb = B["wg"], B["wb"]
-    for d in range(1, ZL):
-        z = up(zl, d, ZL)
-        send(wb.at[me], wg.at[y, c, x, zl], "w1", d - 1, dev(zl_=z))
-    for d in range(1, X):
-        part = gown.at[seg(down(x, d, X) * C + c)]
-        got(part, "fx0", d - 1)
-        send(part, part, "fc0", d, sib)
+    CWs, CWr, wg = B["CWs"], B["CWr"], B["wg"]
+    for b in range(bpd):
+        CWs[b, 0] = cot[:, b * tb:(b + 1) * tb]
+        CWs[b, 1] = B["wb"][me]
+    CWr[zl] = CWs[zl]
+    got(gown.at[pl.ds(0, X - 1), 0], "fx0", 0)
+    send(gown.at[:, c], gown.at[:, c], "fc0", 0, sib)
     loads[3].wait()
     for cp in to_smem:
         cp.wait()
-    acc = tuple(ftab[2 * bpd, b] * dot(gown[me * bpd + b], tv[b], 1, 1) for b in range(bpd))
+    acc = tuple(ftab[2 * bpd, b] * dot(gown[x, c, b], tv[b], 1, 1) for b in range(bpd))
 
     def forward(g, half, i, acc):
         acc = list(acc)
         for j in range(C * PER):
-            m = i * C + j // PER
             k = (half * Q + i * C) * PER + j
-            out = dot(g[m * bpd + itab[1, k]], tv[itab[0, k]], 1, 1)
+            out = dot(g[i, j // PER, itab[1, k]], tv[itab[0, k]], 1, 1)
             for b in range(bpd):
                 acc[b] = acc[b] + ftab[b, k] * out
         return tuple(acc)
 
-    for d in range(1, ZL):
-        got(wg.at[y, c, x, down(zl, d, ZL)], "w1", d - 1)
+    got(goth.at[x, c], "fz", 0)
     for d in range(1, X):
-        send(wg.at[y, c, x], wg.at[y, c, x], "w2", d - 1, dev(x_=up(x, d, X)))
-    got(goth.at[mine], "fz", 0)
+        send(goth.at[x, c], goth.at[x, c], "fx1", d - 1, dev(x_=up(x, d, X)))
+    send_all([(CWs.at[z], CWr.at[zl], dev(zl_=z)) for z in zs], CWr.at[pl.ds(0, ZL - 1)], "cw")
+    got(gown.at[:, co], "fc0", 0)
+    acc = lax.fori_loop(0, Q // C, lambda i, a: forward(gown, zh, i, a), acc)
+    fc1 = [(goth.at[x, c], goth.at[x, c], sib)]
     for d in range(1, X):
-        send(goth.at[mine], goth.at[mine], "fx1", d - 1, dev(x_=up(x, d, X)))
-    send(goth.at[mine], goth.at[mine], "fc1", 0, sib)
-    for d in range(1, ZL):
-        z = up(zl, d, ZL)
-        send(B["cb"].at[z], B["ct"].at[zl], "ct", d - 1, dev(zl_=z))
-    for d in range(X):
-        got(gown.at[seg(down(x, d, X) * C + co)], "fc0", d)
-    acc = lax.fori_loop(0, Q // C, lambda i, a: forward(gown, zh, i, a), acc)
-    for d in range(1, X):
-        got(wg.at[y, c, down(x, d, X)], "w2", d - 1)
+        part = goth.at[down(x, d, X), c]
+        got(part, "fx1", d - 1)
+        fc1.append((part, part, sib))
+    send_all(fc1, goth.at[:, c], "fc1")
+    if ZL > 1:
+        got(CWr.at[pl.ds(0, ZL - 1)], "cw", 0)
+    wg[y, c, x] = CWr[:, 1]
+    part = wg.at[y, c, x]
+    send_all([(part, part, dev(x_=v)) for v in xs], wg.at[y, c, pl.ds(0, X - 1)], "w2")
+    ctT, AT = B["ctT"], B["AT"]
+    ctT[y] = CWr[:, 0].reshape(rows, tb).astype(F32).T.astype(BF)
+    ys = [up(y, d, Y) for d in range(1, Y)]
+    send_all([(ctT.at[y], ctT.at[y], dev(y_=v)) for v in ys], ctT.at[pl.ds(0, Y - 1)], "cty")
+    got(goth.at[:, co], "fc1", 0)
+    acc = lax.fori_loop(0, Q // C, lambda i, a: forward(goth, zo, i, a), acc)
+
+    A = B["A"]
+    for b in range(bpd):
+        B["aggb"][b] = acc[b].astype(BF)
+    A[zl] = B["aggb"][zl]
+    send_all([(B["aggb"].at[z], A.at[zl], dev(zl_=z)) for z in zs], A.at[pl.ds(0, ZL - 1)], "ag")
+    got(wg.at[y, c, pl.ds(0, X - 1)], "w2", 0)
     y_up, y_down, y_far = up(y, 1, Y), down(y, 1, Y), up(y, 2, Y)
     send(wg.at[y, c], wg.at[y, c], "w4", 0, dev(y_=y_up))
     if Y > 2:
         send(wg.at[y, c], wg.at[y, c], "w4", 1, dev(y_=y_down))
     send(wg.at[y, c], wg.at[y, c], "w3", 0, sib)
-    for d in range(1, X):
-        part = goth.at[seg(down(x, d, X) * C + c)]
-        got(part, "fx1", d - 1)
-        send(part, part, "fc1", d, sib)
-    for d in range(1, ZL):
-        got(B["ct"].at[down(zl, d, ZL)], "ct", d - 1)
-    ctT, AT = B["ctT"], B["AT"]
-    ctT[y] = B["ct"][...].reshape(rows, tb).astype(F32).T.astype(BF)
+    if ZL > 1:
+        got(A.at[pl.ds(0, ZL - 1)], "ag", 0)
+
+    a2 = A[...].reshape(rows, tb)
+    AT[y] = a2.astype(F32).T.astype(BF)
     for d in range(1, Y):
-        send(ctT.at[y], ctT.at[y], "cty", d - 1, dev(y_=up(y, d, Y)))
-    for d in range(X):
-        got(goth.at[seg(down(x, d, X) * C + co)], "fc1", d)
-    acc = lax.fori_loop(0, Q // C, lambda i, a: forward(goth, zo, i, a), acc)
-
-    A = B["A"]
-    for b in range(bpd):
-        B["aggb"][b] = acc[b].astype(BF)
-    A[zl] = B["aggb"][zl]
-    for d in range(1, ZL):
-        z = up(zl, d, ZL)
-        send(B["aggb"].at[z], A.at[zl], "ag", d - 1, dev(zl_=z))
+        send(AT.at[y], AT.at[y], "agy", d - 1, dev(y_=up(y, d, Y)))
+
+    def weight_of(y_, i):
+        return jnp.concatenate([wg[y_, e, i].reshape(rows, qw) for e in range(C)], axis=1)
+
+    preT, gpT = B["preT"], B["gpT"]
+    got(wg.at[y, co], "w3", 0)
+    for i in range(X):
+        preT[i] = dot(AT[y], weight_of(y, i), 1, 0)
     half = X // 2
     got(wg.at[y_down, c], "w4", 0)
     send(wg.at[y_down, c], wg.at[y_down, c], "w3", 1, sib)
@@ -287,35 +289,19 @@
         part = wg.at[y_down, c, pl.ds(0, half)]
         send(part, part, "w5", 0, dev(y_=y_up))
         got(wg.at[y_up, c], "w4", 1)
-        send(wg.at[y_up, c], wg.at[y_up, c], "w3", 2, sib)
         part = wg.at[y_up, c, pl.ds(half, half)]
         send(part, part, "w5", 1, dev(y_=y_down))
-    for d in range(1, ZL):
-        got(A.at[down(zl, d, ZL)], "ag", d - 1)
-
-    a2 = A[...].reshape(rows, tb)
-    AT[y] = a2.astype(F32).T.astype(BF)
-    for d in range(1, Y):
-        send(AT.at[y], AT.at[y], "agy", d - 1, dev(y_=up(y, d, Y)))
-
-    def weight_of(y_, i):
-        return jnp.concatenate([wg[y_, e, i].reshape(rows, qw) for e in range(C)], axis=1)
-
-    preT, gpT = B["preT"], B["gpT"]
-    got(wg.at[y, co], "w3", 0)
-    for i in range(X):
-        preT[i] = dot(AT[y], weight_of(y, i), 1, 0)
-    if Y > 2:
-        got(wg.at[y_far, c, pl.ds(0, half)], "w5", 0)
-        got(wg.at[y_far, c, pl.ds(half, half)], "w5", 1)
-        send(wg.at[y_far, c], wg.at[y_far, c], "w3", 3, sib)
-    for d in range(1, Y):
-        got(ctT.at[down(y, d, Y)], "cty", d - 1)
+        send(wg.at[y_up, c], wg.at[y_up, c], "w3", 2, sib)
+    got(ctT.at[pl.ds(0, Y - 1)], "cty", 0)
     order = [(1, 1), (3, 2), (2, 3)] if Y > 2 else [(1, 1)]
     for n, (d, at) in enumerate(order):
         y_ = down(y, d, Y)
+        if d == 2:
+            got(wg.at[y_far, c, pl.ds(0, half)], "w5", 0)
+            got(wg.at[y_far, c, pl.ds(half, half)], "w5", 1)
+            send(wg.at[y_far, c], wg.at[y_far, c], "w3", 3, sib)
+        got(AT.at[y_], "agy", d - 1)
         got(wg.at[y_, co], "w3", at)
-        got(AT.at[y_], "agy", d - 1)
         for i in range(X):
             pre = preT[i] + dot(AT[y_], weight_of(y_, i), 1, 0)
             preT[i] = pre
@@ -334,9 +320,7 @@
     gab, GA = B["gab"], B["GA"]
     gab[...] = ga.astype(BF).reshape(ZL, rb, tb)
     GA[zl] = gab[zl]
-    for d in range(1, ZL):
-        z = up(zl, d, ZL)
-        send(gab.at[z], GA.at[zl], "ga", d - 1, dev(zl_=z))
+    send_all([(gab.at[z], GA.at[zl], dev(zl_=z)) for z in zs], GA.at[pl.ds(0, ZL - 1)], "ga")
 
     PS, PO, PR = B["PS"], B["PO"], B["PR"]
     for i in range(X):
@@ -349,9 +333,12 @@
     for d in range(1, X):
         x_ = up(x, d, X)
         DXs[d - 1] = (PO[x_] + PR[x_].astype(F32)).astype(BF)
-        send(DXs.at[d - 1], DXr.at[d - 1], "dx", d - 1, dev(x_=x_))
-    for d in range(1, ZL):
-        got(GA.at[down(zl, d, ZL)], "ga", d - 1)
+    send_all([(DXs.at[n], DXr.at[n], dev(x_=v)) for n, v in enumerate(xs)], DXr, "dx")
+    ADs, ADr = B["ADs"], B["ADr"]
+    pre = preT[y]
+    ADs[:, 0] = (pre * jax.nn.sigmoid(pre)).T.astype(BF).reshape(ZL, rb, tb)
+    if ZL > 1:
+        got(GA.at[pl.ds(0, ZL - 1)], "ga", 0)
 
     def backward(half, m):
         outs = [None] * bpd
@@ -384,16 +371,18 @@
     whole = pl.ds(0, bpd)
 
     def to_x(n, at=whole, i=0):
-        for d in range(1, X):
-            x_ = up(x, d, X)
-            EXs[n][d - 1, at] = (Dkeep[n][x_, at] + Drec[n][x_, at].astype(F32)).astype(BF)
-            send(EXs[n].at[d - 1, at], EXr[n].at[d - 1, at], "e%d" % n, i * (X - 1) + d - 1, dev(x_=x_))
+        for d, v in enumerate(xs):
+            EXs[n][d, at] = (Dkeep[n][v, at] + Drec[n][v, at].astype(F32)).astype(BF)
+        send_all(
+            [(EXs[n].at[d, at], EXr[n].at[d, at], dev(x_=v)) for d, v in enumerate(xs)],
+            EXr[n].at[:, at], "e%d" % n, i,
+        )
 
     def from_x(n, at=whole, i=0):
+        got(EXr[n].at[:, at], "e%d" % n, i)
         total = Dkeep[n][x, at] + Drec[n][x, at].astype(F32)
-        for d in range(1, X):
-            got(EXr[n].at[d - 1, at], "e%d" % n, i * (X - 1) + d - 1)
-            total = total + EXr[n][d - 1, at].astype(F32)
+        for d in range(X - 1):
+            total = total + EXr[n][d, at].astype(F32)
         return total
 
     contribute(zo, co, Dsib[0])
@@ -403,32 +392,25 @@
     got(Drec[0], "d0", 0)
     for i in range(parts):
         to_x(0, cut(i), i)
-    S32, Sb, DZr = B["S32"], B["Sb"], B["DZr"]
+    S32 = B["S32"]
+    got(DXr, "dx", 0)
     total = PO[x] + PR[x].astype(F32)
-    for d in range(1, X):
-        got(DXr.at[d - 1], "dx", d - 1)
-        total = total + DXr[d - 1].astype(F32)
+    for d in range(X - 1):
+        total = total + DXr[d].astype(F32)
     S32[...] = total
-    Sb[...] = total.astype(BF)
-    for d in range(1, ZL):
-        z = up(zl, d, ZL)
-        send(Sb.at[z], DZr.at[d - 1], "dz", d - 1, dev(zl_=z))
+    ADs[:, 1] = total.astype(BF)
+    ADr[zl] = ADs[zl]
+    send_all([(ADs.at[z], ADr.at[zl], dev(zl_=z)) for z in zs], ADr.at[pl.ds(0, ZL - 1)], "ad")
     contribute(zh, co, Dsib[1])
     send(Dsib[1], Drec[1], "d1", 0, sib)
-    actb, actr = B["actb"], B["actr"]
-    pre = preT[y]
-    actb[...] = (pre * jax.nn.sigmoid(pre)).T.astype(BF).reshape(ZL, rb, tb)
-    actr[zl] = actb[zl]
-    for d in range(1, ZL):
-        z = up(zl, d, ZL)
-        send(actb.at[z], actr.at[zl], "act", d - 1, dev(zl_=z))
     contribute(zh, c, Dkeep[1])
     for b in range(bpd):
         Dkeep[1][x, b] = ftab[2 * bpd, b] * dot(GA[b], tv[b], 1, 0)
     total = S32[zl]
+    if ZL > 1:
+        got(ADr.at[pl.ds(0, ZL - 1)], "ad", 0)
     for d in range(1, ZL):
-        got(DZr.at[d - 1], "dz", d - 1)
-        total = total + DZr[d - 1].astype(F32)
+        total = total + ADr[down(zl, d, ZL), 1].astype(F32)
     Ts, Tr, OutW = B["Ts"], B["Tr"], B["OutW"]
     Ts[...] = total
     send(Ts, Tr, "dt", 0, anti)
@@ -439,28 +421,24 @@
         send(FZs.at[at], FZr.at[at], "gz", i, anti)
     got(Drec[1], "d1", 0)
     to_x(1)
-    for d in range(1, ZL):
-        got(actr.at[down(zl, d, ZL)], "act", d - 1)
-    for b in range(bpd):
-        act_o[:, b * tb:(b + 1) * tb] = actr[b]
+    for b in range(bpd):
+        act_o[:, b * tb:(b + 1) * tb] = ADr[b, 0]
     got(Tr, "dt", 0)
     OutW[me] = Ts[...] + Tr[...]
     others = [(d, e) for d in range(X) for e in range(C) if d or e]
-    for n, (d, e) in enumerate(others):
-        to = dev(x_=up(x, d, X), c_=(co if e else c))
-        send(OutW.at[me], OutW.at[me], "ow", n, to)
+    tos = [dev(x_=up(x, d, X), c_=(co if e else c)) for d, e in others]
+    send_all([(OutW.at[me], OutW.at[me], to) for to in tos], OutW.at[pl.ds(0, Q - 1)], "ow")
     own = from_x(1)
-    for n, (d, e) in enumerate(others):
-        got(OutW.at[down(x, d, X) * C + (co if e else c)], "ow", n)
+    got(OutW.at[pl.ds(0, Q - 1)], "ow", 0)
     for q in range(Q):
         gw_o[:, q * qw:(q + 1) * qw] = OutW[q]
+    for cp in sent:
+        cp.wait_send()
     for i in range(parts):
         got(FZr.at[cut(i)], "gz", i)
     own = (own + FZr[...].astype(F32)).astype(BF)
     for b in range(bpd):
         gf_o[:, b * tb:(b + 1) * tb] = own[b]
-    for cp in sent:
-        cp.wait_send()
 
 
 def on_device(cfg, features_t, tile_dst, tile_src, tile_edges, tile_values, weight, cotangent):

time: 80.5 us -> 83.5 us (1.037); the launches traced: 79 us -> 83.3 us
  Pallas kernels: 76.5 us -> 80.8 us
    pallas_call x1, Pallas kernels: 76.5 us -> 80.8 us  [on_device(): pl.pallas_call(kernel, out_shape=outs, in_specs=[hbm] * 7, out_specs=(vm,...]
where the time goes in v5:
time: 83.5 us; the launch traced here: 83.3 us
  Pallas kernels  80.8 us (97%)
  local copies, waits for them, and re-layouts  1.92 us (2%)
    pallas_call x1, Pallas kernels, on_device(): pl.pallas_call(kernel, out_shape=outs, in_specs=[hbm] * 7, out_specs=(vm,...  80.8 us
    unnamed x3, local copies, waits for them, and re-layouts  1.92 us

profile of v5, /device:TPU:1, one launch (start us, length us, event | category | flops | bytes accessed | tf_op | source)
XLA Modules:
  0.0 83.3 jit_solution(8780345136204687612)
XLA Ops:
  0.6 80.8 %graph_conv.1 = (bf16[32,1024]{1,0:T(8,128)(2,1)S(1)}, f32[32,1024]{1,0:T(8,128)S(1)}, bf16[32,1024]{1,0:T(8,128)(2,1)S(1)}) custom-call(bf16[32,1024]{1,0:T(8,128)(2,1)} %feat_hbm.1, bf16[64,128,128]{2,1,0:T(8,128)(2,1)} %tv_hbm.1, bf16[32,1024]{1,0:T(8,128)(2,1)} %w_hbm.1, bf16[32,1024]{1,0:T(8,128)(2,1)} %cot_hbm.1, s32[1,64]{1,0:T(1,128)} %bitcast.3, ...), custom_call_target="tpu_custom_call" | custom-call | tf_op jit(solution)/shard_map/graph_conv/pallas_call | solution.py:455
  81.4 0.6 copy.13
  82.0 0.6 copy.15
  82.7 0.7 copy.14

commit v6 on v5

--- a/solution.py
+++ b/solution.py
@@ -38,8 +38,8 @@
         gown=((X, C, bpd, rb, tb), BF),
         goth=((X, C, bpd, rb, tb), BF),
         tv=((nt, tb, tb), BF),
-        CWs=((ZL, 2, rb, qw), BF),
-        CWr=((ZL, 2, rb, qw), BF),
+        cb=((bpd, rb, tb), BF),
+        ct=((ZL, rb, tb), BF),
         wb=((Q, rb, qw), BF),
         wg=((Y, C, X, ZL, rb, qw), BF),
         aggb=((bpd, rb, tb), BF),
@@ -75,7 +75,7 @@
         FZr=((bpd, rb, tb), BF),
     )
     sems = dict(
-        fz=1, fx0=1, fx1=x1, fc0=1, fc1=1, cw=1, w2=1, w3=Y, w4=2, w5=2, cty=1, ag=1, agy=y1, ga=1,
+        fz=1, fx0=1, fx1=x1, fc0=1, fc1=1, w1=1, ct=1, w2=1, w3=Y, w4=2, w5=2, cty=1, ag=1, agy=y1, ga=1,
         p=1, dx=1, ad=1, dt=1, ow=1, d0=1, d1=1, e0=2, e1=1, gz=2,
     )
     smem = dict(itab=((8, nk), jnp.int32), ftab=((2 * bpd + 8, nk), F32))
@@ -192,12 +192,18 @@
     loads[0].wait()
     for b in range(bpd):
         gown[x, c, b] = feat[:, b * tb:(b + 1) * tb]
+    loads[1].wait()
+    wg, wb = B["wg"], B["wb"]
+    for q in range(Q):
+        wb[q] = w[:, q * qw:(q + 1) * qw]
+    wg[y, c, x, zl] = wb[me]
     pl.semaphore_wait(barrier, len(partners))
 
     xs = [up(x, d, X) for d in range(1, X)]
     zs = [up(zl, d, ZL) for d in range(1, ZL)]
     send(gown.at[x, c], goth.at[x, c], "fz", 0, anti)
     send_all([(gown.at[x, c], gown.at[x, c], dev(x_=v)) for v in xs], gown.at[pl.ds(0, X - 1), 0], "fx0")
+    send_all([(wb.at[me], wg.at[y, c, x, zl], dev(zl_=z)) for z in zs], wg.at[y, c, x, pl.ds(0, ZL - 1)], "w1")
     for ld in loads[4:]:
         ld.wait()
     tables(bpd, B["dv"][...], B["sv"][...], B["ev"][...], B["itv"], B["ftv"])
@@ -207,15 +213,11 @@
     ]
     for cp in to_smem:
         cp.start()
-    loads[1].wait()
     loads[2].wait()
-    for q in range(Q):
-        B["wb"][q] = w[:, q * qw:(q + 1) * qw]
-    CWs, CWr, wg = B["CWs"], B["CWr"], B["wg"]
-    for b in range(bpd):
-        CWs[b, 0] = cot[:, b * tb:(b + 1) * tb]
-        CWs[b, 1] = B["wb"][me]
-    CWr[zl] = CWs[zl]
+    cb, ct = B["cb"], B["ct"]
+    for b in range(bpd):
+        cb[b] = cot[:, b * tb:(b + 1) * tb]
+    ct[zl] = cb[zl]
     got(gown.at[pl.ds(0, X - 1), 0], "fx0", 0)
     send(gown.at[:, c], gown.at[:, c], "fc0", 0, sib)
     loads[3].wait()
@@ -232,56 +234,42 @@
                 acc[b] = acc[b] + ftab[b, k] * out
         return tuple(acc)
 
+    part = wg.at[y, c, x]
+    if ZL > 1:
+        got(wg.at[y, c, x, pl.ds(0, ZL - 1)], "w1", 0)
+    send_all([(part, part, dev(x_=v)) for v in xs], wg.at[y, c, pl.ds(0, X - 1)], "w2")
     got(goth.at[x, c], "fz", 0)
     for d in range(1, X):
         send(goth.at[x, c], goth.at[x, c], "fx1", d - 1, dev(x_=up(x, d, X)))
-    send_all([(CWs.at[z], CWr.at[zl], dev(zl_=z)) for z in zs], CWr.at[pl.ds(0, ZL - 1)], "cw")
-    got(gown.at[:, co], "fc0", 0)
-    acc = lax.fori_loop(0, Q // C, lambda i, a: forward(gown, zh, i, a), acc)
-    fc1 = [(goth.at[x, c], goth.at[x, c], sib)]
-    for d in range(1, X):
-        part = goth.at[down(x, d, X), c]
-        got(part, "fx1", d - 1)
-        fc1.append((part, part, sib))
-    send_all(fc1, goth.at[:, c], "fc1")
-    if ZL > 1:
-        got(CWr.at[pl.ds(0, ZL - 1)], "cw", 0)
-    wg[y, c, x] = CWr[:, 1]
-    part = wg.at[y, c, x]
-    send_all([(part, part, dev(x_=v)) for v in xs], wg.at[y, c, pl.ds(0, X - 1)], "w2")
-    ctT, AT = B["ctT"], B["AT"]
-    ctT[y] = CWr[:, 0].reshape(rows, tb).astype(F32).T.astype(BF)
-    ys = [up(y, d, Y) for d in range(1, Y)]
-    send_all([(ctT.at[y], ctT.at[y], dev(y_=v)) for v in ys], ctT.at[pl.ds(0, Y - 1)], "cty")
-    got(goth.at[:, co], "fc1", 0)
-    acc = lax.fori_loop(0, Q // C, lambda i, a: forward(goth, zo, i, a), acc)
-
-    A = B["A"]
-    for b in range(bpd):
-        B["aggb"][b] = acc[b].astype(BF)
-    A[zl] = B["aggb"][zl]
-    send_all([(B["aggb"].at[z], A.at[zl], dev(zl_=z)) for z in zs], A.at[pl.ds(0, ZL - 1)], "ag")
+    copy(goth.at[x, c], goth.at[x, c], "fc1", 0, sib).start()
+    send_all([(cb.at[z], ct.at[zl], dev(zl_=z)) for z in zs], ct.at[pl.ds(0, ZL - 1)], "ct")
     got(wg.at[y, c, pl.ds(0, X - 1)], "w2", 0)
     y_up, y_down, y_far = up(y, 1, Y), down(y, 1, Y), up(y, 2, Y)
     send(wg.at[y, c], wg.at[y, c], "w4", 0, dev(y_=y_up))
     if Y > 2:
         send(wg.at[y, c], wg.at[y, c], "w4", 1, dev(y_=y_down))
     send(wg.at[y, c], wg.at[y, c], "w3", 0, sib)
+    got(gown.at[:, co], "fc0", 0)
+    acc = lax.fori_loop(0, Q // C, lambda i, a: forward(gown, zh, i, a), acc)
+    for d in range(1, X):
+        part = goth.at[down(x, d, X), c]
+        got(part, "fx1", d - 1)
+        copy(part, part, "fc1", 0, sib).start()
+    sent.append(copy(goth.at[:, c], goth.at[:, c], "fc1", 0, sib))
     if ZL > 1:
-        got(A.at[pl.ds(0, ZL - 1)], "ag", 0)
-
-    a2 = A[...].reshape(rows, tb)
-    AT[y] = a2.astype(F32).T.astype(BF)
-    for d in range(1, Y):
-        send(AT.at[y], AT.at[y], "agy", d - 1, dev(y_=up(y, d, Y)))
-
-    def weight_of(y_, i):
-        return jnp.concatenate([wg[y_, e, i].reshape(rows, qw) for e in range(C)], axis=1)
-
-    preT, gpT = B["preT"], B["gpT"]
-    got(wg.at[y, co], "w3", 0)
-    for i in range(X):
-        preT[i] = dot(AT[y], weight_of(y, i), 1, 0)
+        got(ct.at[pl.ds(0, ZL - 1)], "ct", 0)
+    ctT, AT = B["ctT"], B["AT"]
+    ctT[y] = ct[...].reshape(rows, tb).astype(F32).T.astype(BF)
+    ys = [up(y, d, Y) for d in range(1, Y)]
+    send_all([(ctT.at[y], ctT.at[y], dev(y_=v)) for v in ys], ctT.at[pl.ds(0, Y - 1)], "cty")
+    got(goth.at[:, co], "fc1", 0)
+    acc = lax.fori_loop(0, Q // C, lambda i, a: forward(goth, zo, i, a), acc)
+
+    A = B["A"]
+    for b in range(bpd):
+        B["aggb"][b] = acc[b].astype(BF)
+    A[zl] = B["aggb"][zl]
+    send_all([(B["aggb"].at[z], A.at[zl], dev(zl_=z)) for z in zs], A.at[pl.ds(0, ZL - 1)], "ag")
     half = X // 2
     got(wg.at[y_down, c], "w4", 0)
     send(wg.at[y_down, c], wg.at[y_down, c], "w3", 1, sib)
@@ -292,6 +280,21 @@
         part = wg.at[y_up, c, pl.ds(half, half)]
         send(part, part, "w5", 1, dev(y_=y_down))
         send(wg.at[y_up, c], wg.at[y_up, c], "w3", 2, sib)
+    if ZL > 1:
+        got(A.at[pl.ds(0, ZL - 1)], "ag", 0)
+
+    a2 = A[...].reshape(rows, tb)
+    AT[y] = a2.astype(F32).T.astype(BF)
+    for d in range(1, Y):
+        send(AT.at[y], AT.at[y], "agy", d - 1, dev(y_=up(y, d, Y)))
+
+    def weight_of(y_, i):
+        return jnp.concatenate([wg[y_, e, i].reshape(rows, qw) for e in range(C)], axis=1)
+
+    preT, gpT = B["preT"], B["gpT"]
+    got(wg.at[y, co], "w3", 0)
+    for i in range(X):
+        preT[i] = dot(AT[y], weight_of(y, i), 1, 0)
     got(ctT.at[pl.ds(0, Y - 1)], "cty", 0)
     order = [(1, 1), (3, 2), (2, 3)] if Y > 2 else [(1, 1)]
     for n, (d, at) in enumerate(order):
@@ -373,10 +376,8 @@
     def to_x(n, at=whole, i=0):
         for d, v in enumerate(xs):
             EXs[n][d, at] = (Dkeep[n][v, at] + Drec[n][v, at].astype(F32)).astype(BF)
-        send_all(
-            [(EXs[n].at[d, at], EXr[n].at[d, at], dev(x_=v)) for d, v in enumerate(xs)],
-            EXr[n].at[:, at], "e%d" % n, i,
-        )
+            copy(EXs[n].at[d, at], EXr[n].at[d, at], "e%d" % n, i, dev(x_=v)).start()
+        sent.append(copy(EXr[n].at[:, at], EXr[n].at[:, at], "e%d" % n, i, sib))
 
     def from_x(n, at=whole, i=0):
         got(EXr[n].at[:, at], "e%d" % n, i)

time: 83.5 us -> 79.9 us (0.957); the launches traced: 83.3 us -> 78.7 us
  Pallas kernels: 80.8 us -> 76.2 us
    pallas_call x1, Pallas kernels: 80.8 us -> 76.2 us  [on_device(): pl.pallas_call(kernel, out_shape=outs, in_specs=[hbm] * 7, out_specs=(vm,...]
where the time goes in v6:
time: 79.9 us; the launch traced here: 78.7 us
  Pallas kernels  76.2 us (95%)
  local copies, waits for them, and re-layouts  1.92 us (2%)
    pallas_call x1, Pallas kernels, on_device(): pl.pallas_call(kernel, out_shape=outs, in_specs=[hbm] * 7, out_specs=(vm,...  76.2 us
    unnamed x3, local copies, waits for them, and re-layouts  1.92 us

profile of v6, /device:TPU:1, one launch (start us, length us, event | category | flops | bytes accessed | tf_op | source)
XLA Modules:
  0.0 78.7 jit_solution(9112949580199495544)
XLA Ops:
  0.6 76.2 %graph_conv.1 = (bf16[32,1024]{1,0:T(8,128)(2,1)S(1)}, f32[32,1024]{1,0:T(8,128)S(1)}, bf16[32,1024]{1,0:T(8,128)(2,1)S(1)}) custom-call(bf16[32,1024]{1,0:T(8,128)(2,1)} %feat_hbm.1, bf16[64,128,128]{2,1,0:T(8,128)(2,1)} %tv_hbm.1, bf16[32,1024]{1,0:T(8,128)(2,1)} %w_hbm.1, bf16[32,1024]{1,0:T(8,128)(2,1)} %cot_hbm.1, s32[1,64]{1,0:T(1,128)} %bitcast.3, ...), custom_call_target="tpu_custom_call" | custom-call | tf_op jit(solution)/shard_map/graph_conv/pallas_call | solution.py:456
  76.8 0.6 copy.13
  77.4 0.6 copy.15
  78.1 0.7 copy.14

commit v7 on v6

--- a/solution.py
+++ b/solution.py
@@ -16,6 +16,10 @@
 
 def dot(a, b, ca, cb):
     return lax.dot_general(a, b, (((ca,), (cb,)), ((), ())), preferred_element_type=F32)
+
+
+def groups(n):
+    return 2 if n % 2 == 0 else 1
 
 
 def shapes(cfg, rb, tb, nt):
@@ -45,7 +49,7 @@
         aggb=((bpd, rb, tb), BF),
         A=((ZL, rb, tb), BF),
         ctT=((Y, tb, rb * ZL), BF),
-        AT=((Y, tb, rb * ZL), BF),
+        AT=((Y, groups(ZL), tb, rb * ZL // groups(ZL)), BF),
         preT=((X, tb, C * qw), F32),
         gpT=((Q, tb, qw), BF),
         ADs=((ZL, 2, rb, tb), BF),
@@ -75,7 +79,7 @@
         FZr=((bpd, rb, tb), BF),
     )
     sems = dict(
-        fz=1, fx0=1, fx1=x1, fc0=1, fc1=1, w1=1, ct=1, w2=1, w3=Y, w4=2, w5=2, cty=1, ag=1, agy=y1, ga=1,
+        fz=2, fx0=1, fx1=2 * x1, fc0=1, fc1=2, w1=1, ct=1, w2=1, w3=Y, w4=2, w5=2, cty=1, ag=2, agy=2 * y1, ga=1,
         p=1, dx=1, ad=1, dt=1, ow=1, d0=1, d1=1, e0=2, e1=1, gz=2,
     )
     smem = dict(itab=((8, nk), jnp.int32), ftab=((2 * bpd + 8, nk), F32))
@@ -201,9 +205,16 @@
 
     xs = [up(x, d, X) for d in range(1, X)]
     zs = [up(zl, d, ZL) for d in range(1, ZL)]
-    send(gown.at[x, c], goth.at[x, c], "fz", 0, anti)
+    parts = groups(bpd)
+
+    def cut(i):
+        return pl.ds(i * (bpd // parts), bpd // parts)
+
+    send(gown.at[x, c, cut(0)], goth.at[x, c, cut(0)], "fz", 0, anti)
     send_all([(gown.at[x, c], gown.at[x, c], dev(x_=v)) for v in xs], gown.at[pl.ds(0, X - 1), 0], "fx0")
     send_all([(wb.at[me], wg.at[y, c, x, zl], dev(zl_=z)) for z in zs], wg.at[y, c, x, pl.ds(0, ZL - 1)], "w1")
+    for i in range(1, parts):
+        send(gown.at[x, c, cut(i)], goth.at[x, c, cut(i)], "fz", i, anti)
     for ld in loads[4:]:
         ld.wait()
     tables(bpd, B["dv"][...], B["sv"][...], B["ev"][...], B["itv"], B["ftv"])
@@ -238,10 +249,12 @@
     if ZL > 1:
         got(wg.at[y, c, x, pl.ds(0, ZL - 1)], "w1", 0)
     send_all([(part, part, dev(x_=v)) for v in xs], wg.at[y, c, pl.ds(0, X - 1)], "w2")
-    got(goth.at[x, c], "fz", 0)
-    for d in range(1, X):
-        send(goth.at[x, c], goth.at[x, c], "fx1", d - 1, dev(x_=up(x, d, X)))
-    copy(goth.at[x, c], goth.at[x, c], "fc1", 0, sib).start()
+    for i in range(parts):
+        part = goth.at[x, c, cut(i)]
+        got(part, "fz", i)
+        for d in range(1, X):
+            send(part, part, "fx1", i * (X - 1) + d - 1, dev(x_=up(x, d, X)))
+        copy(part, part, "fc1", i, sib).start()
     send_all([(cb.at[z], ct.at[zl], dev(zl_=z)) for z in zs], ct.at[pl.ds(0, ZL - 1)], "ct")
     got(wg.at[y, c, pl.ds(0, X - 1)], "w2", 0)
     y_up, y_down, y_far = up(y, 1, Y), down(y, 1, Y), up(y, 2, Y)
@@ -251,25 +264,35 @@
     send(wg.at[y, c], wg.at[y, c], "w3", 0, sib)
     got(gown.at[:, co], "fc0", 0)
     acc = lax.fori_loop(0, Q // C, lambda i, a: forward(gown, zh, i, a), acc)
-    for d in range(1, X):
-        part = goth.at[down(x, d, X), c]
-        got(part, "fx1", d - 1)
-        copy(part, part, "fc1", 0, sib).start()
-    sent.append(copy(goth.at[:, c], goth.at[:, c], "fc1", 0, sib))
+    for i in range(parts):
+        for d in range(1, X):
+            part = goth.at[down(x, d, X), c, cut(i)]
+            got(part, "fx1", i * (X - 1) + d - 1)
+            copy(part, part, "fc1", i, sib).start()
+        sent.append(copy(goth.at[:, c, cut(i)], goth.at[:, c, cut(i)], "fc1", i, sib))
     if ZL > 1:
         got(ct.at[pl.ds(0, ZL - 1)], "ct", 0)
     ctT, AT = B["ctT"], B["AT"]
     ctT[y] = ct[...].reshape(rows, tb).astype(F32).T.astype(BF)
     ys = [up(y, d, Y) for d in range(1, Y)]
     send_all([(ctT.at[y], ctT.at[y], dev(y_=v)) for v in ys], ctT.at[pl.ds(0, Y - 1)], "cty")
-    got(goth.at[:, co], "fc1", 0)
+    for i in range(parts):
+        got(goth.at[:, co, cut(i)], "fc1", i)
     acc = lax.fori_loop(0, Q // C, lambda i, a: forward(goth, zo, i, a), acc)
 
     A = B["A"]
     for b in range(bpd):
         B["aggb"][b] = acc[b].astype(BF)
     A[zl] = B["aggb"][zl]
-    send_all([(B["aggb"].at[z], A.at[zl], dev(zl_=z)) for z in zs], A.at[pl.ds(0, ZL - 1)], "ag")
+    ng = groups(ZL)
+    hz = ZL // ng
+    near = lax.div(zl, hz)
+    for z in zs:
+        copy(B["aggb"].at[z], A.at[zl], "ag", (lax.div(z, hz) + near) % ng, dev(zl_=z)).start()
+    ag_sizes = [A.at[pl.ds(0, hz - 1 if n == 0 else hz)] for n in range(ng)]
+    ag_groups = [(n, r) for n, r in enumerate(ag_sizes) if n > 0 or hz > 1]
+    for n, r in ag_groups:
+        sent.append(copy(r, r, "ag", n, sib))
     half = X // 2
     got(wg.at[y_down, c], "w4", 0)
     send(wg.at[y_down, c], wg.at[y_down, c], "w3", 1, sib)
@@ -280,13 +303,18 @@
         part = wg.at[y_up, c, pl.ds(half, half)]
         send(part, part, "w5", 1, dev(y_=y_down))
         send(wg.at[y_up, c], wg.at[y_up, c], "w3", 2, sib)
-    if ZL > 1:
-        got(A.at[pl.ds(0, ZL - 1)], "ag", 0)
-
+
+    for n in range(ng):
+        if n > 0 or hz > 1:
+            got(ag_sizes[n], "ag", n)
+        g = near if n == 0 else 1 - near
+        AT[y, g] = A[pl.ds(g * hz, hz)].reshape(rows // ng, tb).astype(F32).T.astype(BF)
+        for d in range(1, Y):
+            send(AT.at[y, g], AT.at[y, g], "agy", n * (Y - 1) + d - 1, dev(y_=up(y, d, Y)))
     a2 = A[...].reshape(rows, tb)
-    AT[y] = a2.astype(F32).T.astype(BF)
-    for d in range(1, Y):
-        send(AT.at[y], AT.at[y], "agy", d - 1, dev(y_=up(y, d, Y)))
+
+    def nodes_by_rows(y_):
+        return jnp.concatenate([AT[y_, g] for g in range(ng)], axis=1)
 
     def weight_of(y_, i):
         return jnp.concatenate([wg[y_, e, i].reshape(rows, qw) for e in range(C)], axis=1)
@@ -294,7 +322,7 @@
     preT, gpT = B["preT"], B["gpT"]
     got(wg.at[y, co], "w3", 0)
     for i in range(X):
-        preT[i] = dot(AT[y], weight_of(y, i), 1, 0)
+        preT[i] = dot(nodes_by_rows(y), weight_of(y, i), 1, 0)
     got(ctT.at[pl.ds(0, Y - 1)], "cty", 0)
     order = [(1, 1), (3, 2), (2, 3)] if Y > 2 else [(1, 1)]
     for n, (d, at) in enumerate(order):
@@ -303,10 +331,11 @@
             got(wg.at[y_far, c, pl.ds(0, half)], "w5", 0)
             got(wg.at[y_far, c, pl.ds(half, half)], "w5", 1)
             send(wg.at[y_far, c], wg.at[y_far, c], "w3", 3, sib)
-        got(AT.at[y_], "agy", d - 1)
+        for g in range(ng):
+            got(AT.at[y_, near if g == 0 else 1 - near], "agy", g * (Y - 1) + d - 1)
         got(wg.at[y_, co], "w3", at)
         for i in range(X):
-            pre = preT[i] + dot(AT[y_], weight_of(y_, i), 1, 0)
+            pre = preT[i] + dot(nodes_by_rows(y_), weight_of(y_, i), 1, 0)
             preT[i] = pre
             if n == len(order) - 1:
                 sig = jax.nn.sigmoid(pre)
@@ -365,11 +394,6 @@
 
     Dsib, Drec, Dkeep = (B["Dsib0"], B["Dsib1"]), (B["Drec0"], B["Drec1"]), (B["Dkeep0"], B["Dkeep1"])
     EXs, EXr = (B["EXs0"], B["EXs1"]), (B["EXr0"], B["EXr1"])
-
-    parts = 2 if bpd % 2 == 0 else 1
-
-    def cut(i):
-        return pl.ds(i * (bpd // parts), bpd // parts)
 
     whole = pl.ds(0, bpd)
 

time: 79.9 us -> 81.4 us (1.019); the launches traced: 78.7 us -> 81.3 us
  Pallas kernels: 76.2 us -> 78.7 us
    pallas_call x1, Pallas kernels: 76.2 us -> 78.7 us  [on_device(): pl.pallas_call(kernel, out_shape=outs, in_specs=[hbm] * 7, out_specs=(vm,...]
where the time goes in v7:
time: 81.4 us; the launch traced here: 81.3 us
  Pallas kernels  78.7 us (97%)
  local copies, waits for them, and re-layouts  1.92 us (2%)
    pallas_call x1, Pallas kernels, on_device(): pl.pallas_call(kernel, out_shape=outs, in_specs=[hbm] * 7, out_specs=(vm,...  78.7 us
    unnamed x3, local copies, waits for them, and re-layouts  1.92 us

profile of v7, /device:TPU:1, one launch (start us, length us, event | category | flops | bytes accessed | tf_op | source)
XLA Modules:
  0.0 81.3 jit_solution(5705322947304419928)
XLA Ops:
  0.6 78.7 %graph_conv.1 = (bf16[32,1024]{1,0:T(8,128)(2,1)S(1)}, f32[32,1024]{1,0:T(8,128)S(1)}, bf16[32,1024]{1,0:T(8,128)(2,1)S(1)}) custom-call(bf16[32,1024]{1,0:T(8,128)(2,1)} %feat_hbm.1, bf16[64,128,128]{2,1,0:T(8,128)(2,1)} %tv_hbm.1, bf16[32,1024]{1,0:T(8,128)(2,1)} %w_hbm.1, bf16[32,1024]{1,0:T(8,128)(2,1)} %cot_hbm.1, s32[1,64]{1,0:T(1,128)} %bitcast.3, ...), custom_call_target="tpu_custom_call" | custom-call | tf_op jit(solution)/shard_map/graph_conv/pallas_call | solution.py:480
  79.3 0.6 copy.13
  80.0 0.6 copy.15
  80.6 0.7 copy.14

commit v8 on v6

--- a/solution.py
+++ b/solution.py
@@ -388,11 +388,6 @@
 
     contribute(zo, co, Dsib[0])
     send(Dsib[0], Drec[0], "d0", 0, sib)
-    contribute(zo, c, Dkeep[0])
-
-    got(Drec[0], "d0", 0)
-    for i in range(parts):
-        to_x(0, cut(i), i)
     S32 = B["S32"]
     got(DXr, "dx", 0)
     total = PO[x] + PR[x].astype(F32)
@@ -402,11 +397,13 @@
     ADs[:, 1] = total.astype(BF)
     ADr[zl] = ADs[zl]
     send_all([(ADs.at[z], ADr.at[zl], dev(zl_=z)) for z in zs], ADr.at[pl.ds(0, ZL - 1)], "ad")
+    contribute(zo, c, Dkeep[0])
+
+    got(Drec[0], "d0", 0)
+    for i in range(parts):
+        to_x(0, cut(i), i)
     contribute(zh, co, Dsib[1])
     send(Dsib[1], Drec[1], "d1", 0, sib)
-    contribute(zh, c, Dkeep[1])
-    for b in range(bpd):
-        Dkeep[1][x, b] = ftab[2 * bpd, b] * dot(GA[b], tv[b], 1, 0)
     total = S32[zl]
     if ZL > 1:
         got(ADr.at[pl.ds(0, ZL - 1)], "ad", 0)
@@ -420,6 +417,9 @@
         at = cut(i)
         FZs[at] = from_x(0, at, i).astype(BF)
         send(FZs.at[at], FZr.at[at], "gz", i, anti)
+    contribute(zh, c, Dkeep[1])
+    for b in range(bpd):
+        Dkeep[1][x, b] = ftab[2 * bpd, b] * dot(GA[b], tv[b], 1, 0)
     got(Drec[1], "d1", 0)
     to_x(1)
     for b in range(bpd):

time: 79.9 us -> 78.6 us (0.984); the launches traced: 78.7 us -> 78.4 us
  no operation moved by 1% of the time
where the time goes in v8:
time: 78.6 us; the launch traced here: 78.4 us
  Pallas kernels  75.9 us (97%)
  local copies, waits for them, and re-layouts  1.92 us (2%)
    pallas_call x1, Pallas kernels, on_device(): pl.pallas_call(kernel, out_shape=outs, in_specs=[hbm] * 7, out_specs=(vm,...  75.9 us
    unnamed x3, local copies, waits for them, and re-layouts  1.92 us

profile of v8, /device:TPU:1, one launch (start us, length us, event | category | flops | bytes accessed | tf_op | source)
XLA Modules:
  0.0 78.4 jit_solution(16251195445341098652)
XLA Ops:
  0.6 75.9 %graph_conv.1 = (bf16[32,1024]{1,0:T(8,128)(2,1)S(1)}, f32[32,1024]{1,0:T(8,128)S(1)}, bf16[32,1024]{1,0:T(8,128)(2,1)S(1)}) custom-call(bf16[32,1024]{1,0:T(8,128)(2,1)} %feat_hbm.1, bf16[64,128,128]{2,1,0:T(8,128)(2,1)} %tv_hbm.1, bf16[32,1024]{1,0:T(8,128)(2,1)} %w_hbm.1, bf16[32,1024]{1,0:T(8,128)(2,1)} %cot_hbm.1, s32[1,64]{1,0:T(1,128)} %bitcast.3, ...), custom_call_target="tpu_custom_call" | custom-call | tf_op jit(solution)/shard_map/graph_conv/pallas_call | solution.py:456
  76.5 0.6 copy.13
  77.1 0.6 copy.15
  77.8 0.7 copy.14

commit v9 on v7

--- a/solution.py
+++ b/solution.py
@@ -412,11 +412,6 @@
 
     contribute(zo, co, Dsib[0])
     send(Dsib[0], Drec[0], "d0", 0, sib)
-    contribute(zo, c, Dkeep[0])
-
-    got(Drec[0], "d0", 0)
-    for i in range(parts):
-        to_x(0, cut(i), i)
     S32 = B["S32"]
     got(DXr, "dx", 0)
     total = PO[x] + PR[x].astype(F32)
@@ -426,11 +421,13 @@
     ADs[:, 1] = total.astype(BF)
     ADr[zl] = ADs[zl]
     send_all([(ADs.at[z], ADr.at[zl], dev(zl_=z)) for z in zs], ADr.at[pl.ds(0, ZL - 1)], "ad")
+    contribute(zo, c, Dkeep[0])
+
+    got(Drec[0], "d0", 0)
+    for i in range(parts):
+        to_x(0, cut(i), i)
     contribute(zh, co, Dsib[1])
     send(Dsib[1], Drec[1], "d1", 0, sib)
-    contribute(zh, c, Dkeep[1])
-    for b in range(bpd):
-        Dkeep[1][x, b] = ftab[2 * bpd, b] * dot(GA[b], tv[b], 1, 0)
     total = S32[zl]
     if ZL > 1:
         got(ADr.at[pl.ds(0, ZL - 1)], "ad", 0)
@@ -444,6 +441,9 @@
         at = cut(i)
         FZs[at] = from_x(0, at, i).astype(BF)
         send(FZs.at[at], FZr.at[at], "gz", i, anti)
+    contribute(zh, c, Dkeep[1])
+    for b in range(bpd):
+        Dkeep[1][x, b] = ftab[2 * bpd, b] * dot(GA[b], tv[b], 1, 0)
     got(Drec[1], "d1", 0)
     to_x(1)
     for b in range(bpd):

time: 81.4 us -> 79.9 us (0.982)
  Pallas kernels: 78.7 us -> 77.2 us
    pallas_call x1, Pallas kernels: 78.7 us -> 77.2 us  [on_device(): pl.pallas_call(kernel, out_shape=outs, in_specs=[hbm] * 7, out_specs=(vm,...]
where the time goes in v9:
time: 79.9 us; the launch traced here: 79.7 us
  Pallas kernels  77.2 us (97%)
  local copies, waits for them, and re-layouts  1.92 us (2%)
    pallas_call x1, Pallas kernels, on_device(): pl.pallas_call(kernel, out_shape=outs, in_specs=[hbm] * 7, out_specs=(vm,...  77.2 us
    unnamed x3, local copies, waits for them, and re-layouts  1.92 us

profile of v9, /device:TPU:1, one launch (start us, length us, event | category | flops | bytes accessed | tf_op | source)
XLA Modules:
  0.0 79.7 jit_solution(14000176731279230115)
XLA Ops:
  0.6 77.2 %graph_conv.1 = (bf16[32,1024]{1,0:T(8,128)(2,1)S(1)}, f32[32,1024]{1,0:T(8,128)S(1)}, bf16[32,1024]{1,0:T(8,128)(2,1)S(1)}) custom-call(bf16[32,1024]{1,0:T(8,128)(2,1)} %feat_hbm.1, bf16[64,128,128]{2,1,0:T(8,128)(2,1)} %tv_hbm.1, bf16[32,1024]{1,0:T(8,128)(2,1)} %w_hbm.1, bf16[32,1024]{1,0:T(8,128)(2,1)} %cot_hbm.1, s32[1,64]{1,0:T(1,128)} %bitcast.3, ...), custom_call_target="tpu_custom_call" | custom-call | tf_op jit(solution)/shard_map/graph_conv/pallas_call | solution.py:480
  77.8 0.6 copy.13
  78.4 0.6 copy.15
  79.1 0.7 copy.14
